TPU v7x, 128 devices: a whole 4x4x4 slice. The times are simulated.
128 devices in a mesh: tm: 128 (over y, z, x, core).
Axes of the slice: x: 4, y: 4, z: 4, core: 2. Of those that a mesh axis runs over, the one named last changes fastest.
Arguments:
- stream: bfloat16 [262144, 128], P('tm'), may hold values from -160 to 160
- stem_weight: bfloat16 [7, 128, 128], replicated, may hold values from -0.1875 to 0.1875
- stem_bias: float32 [128], replicated, may hold values from -3 to 3
- first_weight: bfloat16 [3, 128, 256], replicated, may hold values from -0.3125 to 0.3125
- deep_weight: bfloat16 [3, 3, 256, 256], replicated, may hold values from -0.21875 to 0.21875
- layer_bias: float32 [4, 256], replicated, may hold values from -3 to 3
- head_weight: bfloat16 [256, 128], replicated, may hold values from -0.375 to 0.375
- head_bias: float32 [128], replicated, may hold values from -3 to 3
- profiles: float32 [4, 4096], replicated, may hold values from 0.25 to 2
- starts: int32 [512], P('tm'), may hold values from 0 to 258048, as said below
- profile_index: int32 [512], P('tm'), may hold values from 0 to 3
- counts: int32 [128], P('tm'), may hold values from 1 to 4, as said below
Outputs:
- embedding: bfloat16 [262144, 128], P('tm')
Inputs may be any that keep to these rules, and one draw needn't show every extreme that they name: `starts`: window slot d * 4 + j belongs to index d of tm; its start is a multiple of 256 from max(0, (d - 1) * 2048) to min((d + 1) * 2048 - 256, 258048). Index d of tm has live windows in its first counts[d] slots; some index has all 4.
All inputs are finite; a program needn't handle non-finite values.
Results may differ from a plain program's by a relative error of at most 0.013.
Values may be sent and summed in bfloat16 or wider, within the bound.
A program may use at most 128 MiB of HBM per device.

v0:
```python
import jax
import jax.numpy as jnp
from jax import lax
from jax.sharding import PartitionSpec as P

norm_epsilon = 1e-05


def padded_2(block, sides, width):
    for axis, dim in sides:
        count = lax.axis_size(axis)
        forward = [(i, i + 1) for i in range(count - 1)]
        backward = [(target, source) for source, target in forward]
        low = lax.ppermute(
            lax.slice_in_dim(block, block.shape[dim] - width, None, axis=dim), axis, forward
        )
        high = lax.ppermute(lax.slice_in_dim(block, 0, width, axis=dim), axis, backward)
        block = jnp.concatenate([low, block, high], axis=dim)
    return block


def shifted(block, axis, distance):
    devices = range(lax.axis_size(axis))
    route = [(i - distance, i) for i in devices if i - distance in devices]
    return lax.ppermute(block, axis, route)


def stem_layer(padded, stem_weight, stem_bias):
    length = padded.shape[0] - stem_weight.shape[0] + 1
    summed = jnp.zeros((length, stem_weight.shape[2]), jnp.float32) + stem_bias
    for k in range(stem_weight.shape[0]):
        summed = summed + jnp.dot(
            padded[k : k + length], stem_weight[k], preferred_element_type=jnp.float32
        )
    return jax.nn.gelu(summed).astype(jnp.bfloat16)


def normalize_window(window_rows):
    values = window_rows.astype(jnp.float32)
    mean_value = jnp.mean(values, axis=0)
    spread = jnp.mean(values * values, axis=0) - mean_value * mean_value
    return ((values - mean_value) * lax.rsqrt(spread + norm_epsilon)).astype(jnp.bfloat16)


def temporal_net(window_rows, first_weight, deep_weight, layer_bias, head_weight, head_bias):
    length = window_rows.shape[0]
    hidden = window_rows
    for layer_index in range(deep_weight.shape[0] + 1):
        kernel = first_weight if layer_index == 0 else deep_weight[layer_index - 1]
        spread = 2**layer_index
        tap_count = kernel.shape[0]
        padded = jnp.pad(hidden, ((spread * (tap_count - 1), 0), (0, 0)))
        summed = jnp.zeros((length, kernel.shape[2]), jnp.float32) + layer_bias[layer_index]
        for k in range(tap_count):
            summed = summed + jnp.dot(
                padded[k * spread : k * spread + length],
                kernel[k],
                preferred_element_type=jnp.float32,
            )
        active = jax.nn.gelu(summed)
        if layer_index > 0:
            active = active + hidden.astype(jnp.float32)
        hidden = active.astype(jnp.bfloat16)
    projected = jnp.dot(hidden, head_weight, preferred_element_type=jnp.float32) + head_bias
    return projected.astype(jnp.bfloat16)


def run_windows(window_slots, live_count, net_params):
    first_weight, deep_weight, layer_bias, head_weight, head_bias = net_params

    def compute_one(slot_index, results):
        window_rows = lax.dynamic_index_in_dim(window_slots, slot_index, 0, keepdims=False)
        normed = normalize_window(window_rows)
        output = temporal_net(normed, first_weight, deep_weight, layer_bias, head_weight, head_bias)
        return lax.dynamic_update_index_in_dim(results, output, slot_index, 0)

    return lax.fori_loop(0, live_count, compute_one, jnp.zeros(window_slots.shape, jnp.bfloat16))


def per_device(
    stream,
    stem_weight,
    stem_bias,
    first_weight,
    deep_weight,
    layer_bias,
    head_weight,
    head_bias,
    profiles,
    starts,
    profile_index,
    counts,
):
    shard_rows = stream.shape[0]
    margin = (stem_weight.shape[0] - 1) // 2
    padded = padded_2(stream, (("tm", 0),), margin)
    features = stem_layer(padded, stem_weight, stem_bias)
    rank_here = lax.axis_index("tm")
    window_length = profiles.shape[1]
    slot_count = starts.shape[0]
    channels = features.shape[1]
    net_params = (first_weight, deep_weight, layer_bias, head_weight, head_bias)
    neighbours = [shifted(features, "tm", offset_by) for offset_by in (1, -1, -2)]
    time_frame = jnp.concatenate([neighbours[0], features, neighbours[1], neighbours[2]], axis=0)
    frame_base = (rank_here - 1) * shard_rows
    window_slots = jnp.stack(
        [
            lax.dynamic_slice_in_dim(time_frame, starts[slot_index] - frame_base, window_length, 0)
            for slot_index in range(slot_count)
        ]
    )
    own_count = counts[0]
    results = run_windows(window_slots, own_count, net_params)
    onehot = (
        profile_index[:, None] == jnp.arange(profiles.shape[0], dtype=jnp.int32)[None, :]
    ).astype(jnp.float32)
    slot_weights = jnp.dot(onehot, profiles, precision=lax.Precision.HIGHEST)

    def add_window(slot_index, running):
        weighted, weight_total = running
        living = (slot_index < own_count).astype(jnp.float32)
        offset = lax.dynamic_index_in_dim(starts, slot_index, 0, keepdims=False) - frame_base
        weight_row = lax.dynamic_index_in_dim(slot_weights, slot_index, 0, keepdims=False) * living
        output = lax.dynamic_index_in_dim(results, slot_index, 0, keepdims=False)
        previous = lax.dynamic_slice_in_dim(weighted, offset, window_length, 0)
        weighted = lax.dynamic_update_slice_in_dim(
            weighted, previous + output.astype(jnp.float32) * weight_row[:, None], offset, 0
        )
        previous_total = lax.dynamic_slice_in_dim(weight_total, offset, window_length, 0)
        weight_total = lax.dynamic_update_slice_in_dim(
            weight_total, previous_total + weight_row, offset, 0
        )
        return (weighted, weight_total)

    initial = (
        jnp.zeros((4 * shard_rows, channels), jnp.float32),
        jnp.zeros((4 * shard_rows,), jnp.float32),
    )
    weighted, weight_total = lax.fori_loop(0, slot_count, add_window, initial)
    summed_rows = weighted[shard_rows : 2 * shard_rows]
    summed_weight = weight_total[shard_rows : 2 * shard_rows]
    for offset_by, quarter in ((-1, 0), (1, 2), (2, 3)):
        first_row = quarter * shard_rows
        arrived_rows, arrived_weight = (
            shifted(
                weighted[first_row : first_row + shard_rows].astype(jnp.bfloat16), "tm", offset_by
            ).astype(jnp.float32),
            shifted(
                weight_total[first_row : first_row + shard_rows].astype(jnp.bfloat16),
                "tm",
                offset_by,
            ).astype(jnp.float32),
        )
        summed_rows = summed_rows + arrived_rows
        summed_weight = summed_weight + arrived_weight
    return (summed_rows / jnp.maximum(summed_weight, 1.0)[:, None]).astype(jnp.bfloat16)


def solution(mesh):
    in_specs = (P("tm", None), P(), P(), P(), P(), P(), P(), P(), P(), P("tm"), P("tm"), P("tm"))
    out_specs = P("tm", None)
    return jax.shard_map(
        per_device, mesh=mesh, in_specs=in_specs, out_specs=out_specs, check_vma=False
    )
```

profile of v0, /device:TPU:24, one launch (start us, length us, event | category | flops | bytes accessed | tf_op | source)
XLA Modules:
  0.0 237.5 jit_solution(17942472434487836995)
XLA Ops:
  2.7 7.9 %collective-permute-start.1 = (bf16[3,128]{1,0:T(4,128)(2,1)S(1)}, bf16[3,128]{1,0:T(4,128)(2,1)S(1)}, u32[]{:S(2)}, u32[]{:S(2)}) collective-permute-start(bf16[3,128]{1,0:T(4,128)(2,1)S(1)} %get-tuple-element.312), channel_id=1, source_target_pairs={{1,0},{2,1},{3,2},{4,3},{5,4},{6,5},{7,6},{8,7},{9,8},{10,9},{11,1... | collective-permute-start | bytes 2312 | tf_op jit(solution)/shard_map/ppermute | solution.py:17
  16.0 1.9 collective-permute-start.2
  17.9 7.9 %collective-permute-start.3 = (bf16[2048,128]{1,0:T(8,128)(2,1)S(1)}, bf16[2048,128]{1,0:T(8,128)(2,1)S(1)}, u32[]{:S(2)}, u32[]{:S(2)}) collective-permute-start(bf16[2048,128]{1,0:T(8,128)(2,1)S(1)} %fusion.118), channel_id=1, source_target_pairs={{1,0},{2,1},{3,2},{4,3},{5,4},{6,5},{7,6},{8,7},{9,8},{10,9},{11,1... | collective-permute-start | bytes 1572872 | tf_op jit(solution)/shard_map/ppermute | solution.py:25
  25.8 1.9 collective-permute-start.4
  31.9 4.8 %collective-permute-done.3 = bf16[2048,128]{1,0:T(8,128)(2,1)S(1)} collective-permute-done((bf16[2048,128]{1,0:T(8,128)(2,1)S(1)}, bf16[2048,128]{1,0:T(8,128)(2,1)S(1)}, u32[]{:S(2)}, u32[]{:S(2)}) %collective-permute-start.3) | collective-permute-done | bytes 524320 | tf_op jit(solution)/shard_map/ppermute | solution.py:25
  36.7 7.0 %collective-permute-done.4 = bf16[2048,128]{1,0:T(8,128)(2,1)S(1)} collective-permute-done((bf16[2048,128]{1,0:T(8,128)(2,1)S(1)}, bf16[2048,128]{1,0:T(8,128)(2,1)S(1)}, u32[]{:S(2)}, u32[]{:S(2)}) %collective-permute-start.4) | collective-permute-done | bytes 524320 | tf_op jit(solution)/shard_map/ppermute | solution.py:25
  45.0 2.2 pad_maximum_fusion
  47.2 2.6 %broadcast_in_dim.28 = bf16[4,4096,128]{2,1,0:T(8,128)(2,1)} broadcast(bf16[]{:T(256)} %constant.124.clone.1), dimensions={} | broadcast | bytes 4194306 | tf_op jit(solution)/shard_map/broadcast_in_dim | solution.py:77
  49.8 26.8 %while.27 = (s32[]{:T(128)}, bf16[4,4096,128]{2,1,0:T(8,128)(2,1)}, s32[]{:T(128)}, f32[4,256]{1,0:T(4,128)S(1)}, bf16[4,4096,128]{2,1,0:T(8,128)(2,1)}, /*index...) while((s32[]{:T(128)}, bf16[4,4096,128]{2,1,0:T(8,128)(2,1)}, ...), condition=%wide.region_3.4_spmd, body=%wide.region_0.3_spmd.sunk | while | flops 5970067968 | bytes 108414632 | solution.py:77
  57.1 3.0 %fusion.227 = bf16[4096,256]{1,0:T(8,128)(2,1)S(1)} fusion(f32[4096,256]{1,0:T(8,128)S(1)} %convolution_add_fusion.24, f32[128]{0:T(128)S(1)} %get-tuple-element.427, f32[128]{0:T(128)S(1)} %get-tuple-element.428, bf16[4,4096,128]{2,1,0:T(8,128)(2,1)} %get-tuple-element.465, s32[]{:T(128)S(6)} %select_n.47, ...), kind=kOutput, calls=%fused_computation.27.clone.1 | convolution fusion | flops 281018368 | bytes 7406596 | tf_op jit(solution)/shard_map/while/body/dot_general | solution.py:55
  67.7 2.7 %convolution_add_fusion.30 = f32[4096,256]{1,0:T(8,128)} fusion(f32[4096,256]{1,0:T(8,128)S(1)} %convolution_add_fusion.29, bf16[4096,256]{1,0:T(8,128)(2,1)S(1)} %fusion.229, bf16[3,3,256,256]{3,2,1,0:T(8,128)(2,1)S(1)} %get-tuple-element.467), kind=kOutput, calls=%fused_computation.5.clone.1 | convolution fusion | flops 537919488 | bytes 10616832 | tf_op jit(solution)/shard_map/while/body/dot_general | solution.py:55
  70.4 5.3 %fusion.230 = bf16[4,4096,128]{2,1,0:T(8,128)(2,1)} fusion(bf16[4,4096,128]{2,1,0:T(8,128)(2,1)} %get-tuple-element.450, s32[]{:T(128)S(6)} %select_n.47, bf16[256,128]{1,0:T(8,128)(2,1)} %get-tuple-element.468, f32[4096,256]{1,0:T(8,128)} %convolution_add_fusion.30, bf16[4096,256]{1,0:T(8,128)(2,1)S(1)} %fusion.229, ...), kind=kOutput, calls=%fused_computation.19.clone.1 | convolution fusion | flops 818937856 | bytes 9634308 | tf_op jit(solution)/shard_map/while/body/dot_general | solution.py:64
  76.6 2.2 broadcast_in_dim.26
  78.8 47.1 %while.28 = (s32[]{:T(128)}, f32[8192,128]{1,0:T(8,128)}, f32[8192]{0:T(1024)S(1)}, s32[4]{0:T(128)S(1)}, s32[]{:T(128)}, /*index=5*/bf16[4,4096,128]{2,1,0:T(8,...) while((s32[]{:T(128)}, f32[8192,128]{1,0:T(8,128)}, ...), condition=%wide.region_5.6_spmd, body=%wide.region_4.5_spmd.sunk | while | flops 1581064 | bytes 9535693 | solution.py:139
  81.7 2.2 fusion.231
  83.9 6.5 %dynamic_update_slice.28 = f32[8192,128]{1,0:T(8,128)} dynamic-update-slice(f32[8192,128]{1,0:T(8,128)} %get-tuple-element.485, f32[4096,128]{1,0:T(8,128)S(1)} %fusion.231, s32[]{:T(128)S(6)} %select_n.48, s32[]{:T(128)} %constant.119.clone.1..sunk.1) | dynamic-update-slice | bytes 4194308 | tf_op jit(solution)/shard_map/while/body/eval_jaxpr/dynamic_update_slice | solution.py:126
  93.5 2.2 fusion.231
  95.7 6.5 %dynamic_update_slice.28 = f32[8192,128]{1,0:T(8,128)} dynamic-update-slice(f32[8192,128]{1,0:T(8,128)} %get-tuple-element.485, f32[4096,128]{1,0:T(8,128)S(1)} %fusion.231, s32[]{:T(128)S(6)} %select_n.48, s32[]{:T(128)} %constant.119.clone.1..sunk.1) | dynamic-update-slice | bytes 4194308 | tf_op jit(solution)/shard_map/while/body/eval_jaxpr/dynamic_update_slice | solution.py:126
  105.3 2.2 fusion.231
  107.5 6.5 %dynamic_update_slice.28 = f32[8192,128]{1,0:T(8,128)} dynamic-update-slice(f32[8192,128]{1,0:T(8,128)} %get-tuple-element.485, f32[4096,128]{1,0:T(8,128)S(1)} %fusion.231, s32[]{:T(128)S(6)} %select_n.48, s32[]{:T(128)} %constant.119.clone.1..sunk.1) | dynamic-update-slice | bytes 4194308 | tf_op jit(solution)/shard_map/while/body/eval_jaxpr/dynamic_update_slice | solution.py:126
  117.1 2.2 fusion.231
  119.3 6.5 %dynamic_update_slice.28 = f32[8192,128]{1,0:T(8,128)} dynamic-update-slice(f32[8192,128]{1,0:T(8,128)} %get-tuple-element.485, f32[4096,128]{1,0:T(8,128)S(1)} %fusion.231, s32[]{:T(128)S(6)} %select_n.48, s32[]{:T(128)} %constant.119.clone.1..sunk.1) | dynamic-update-slice | bytes 4194308 | tf_op jit(solution)/shard_map/while/body/eval_jaxpr/dynamic_update_slice | solution.py:126
  126.0 2.4 %convert.11 = bf16[8192,128]{1,0:T(8,128)(2,1)S(1)} convert(f32[8192,128]{1,0:T(8,128)} %get-tuple-element.262) | non-fusion elementwise | flops 1048576 | bytes 6291456 | tf_op jit(solution)/shard_map/convert.6
  128.5 4.2 %collective-permute-start.5 = (bf16[2048,128]{1,0:T(8,128)(2,1)S(1)}, bf16[2048,128]{1,0:T(8,128)(2,1)S(1)}, u32[]{:S(2)}, u32[]{:S(2)}) collective-permute-start(bf16[2048,128]{1,0:T(8,128)(2,1)S(1)} %get-tuple-element.304), channel_id=1, source_target_pairs={{1,0},{2,1},{3,2},{4,3},{5,4},{6,5},{7,6},{8,7},{9,8},{10,9},{11,1... | collective-permute-start | bytes 1572872 | tf_op jit(solution)/shard_map/ppermute | solution.py:25
  132.7 72.9 %collective-permute-start.6 = (bf16[2048,128]{1,0:T(8,128)(2,1)S(1)}, bf16[2048,128]{1,0:T(8,128)(2,1)S(1)}, u32[]{:S(2)}, u32[]{:S(2)}) collective-permute-start(bf16[2048,128]{1,0:T(8,128)(2,1)S(1)} %get-tuple-element.306), channel_id=1, source_target_pairs={{0,1},{1,2},{2,3},{3,4},{4,5},{5,6},{6,7},{7,8},{8,9},{9,10},{10,1... | collective-permute-start | bytes 1572872 | tf_op jit(solution)/shard_map/ppermute | solution.py:25
  205.7 3.5 %collective-permute-start.7 = (bf16[2048,128]{1,0:T(8,128)(2,1)S(1)}, bf16[2048,128]{1,0:T(8,128)(2,1)S(1)}, u32[]{:S(2)}, u32[]{:S(2)}) collective-permute-start(bf16[2048,128]{1,0:T(8,128)(2,1)S(1)} %get-tuple-element.305), channel_id=1, source_target_pairs={{0,2},{1,3},{2,4},{3,5},{4,6},{5,7},{6,8},{7,9},{8,10},{9,11},{10,... | collective-permute-start | bytes 1572872 | tf_op jit(solution)/shard_map/ppermute | solution.py:25
  209.2 2.1 collective-permute-start.10
  211.4 7.4 %collective-permute-start.8 = (bf16[2048]{0:T(1024)(128)(2,1)S(1)}, bf16[2048]{0:T(1024)(128)(2,1)S(1)}, u32[]{:S(2)}, u32[]{:S(2)}) collective-permute-start(bf16[2048]{0:T(1024)(128)(2,1)S(1)} %get-tuple-element.313), channel_id=1, source_target_pairs={{1,0},{2,1},{3,2},{4,3},{5,4},{6,5},{7,6},{8,7},{9,8},{10,9},{11,1... | collective-permute-start | bytes 12296 | tf_op jit(solution)/shard_map/ppermute | solution.py:25
  218.7 7.2 %collective-permute-done.10 = bf16[2048]{0:T(1024)(128)(2,1)S(1)} collective-permute-done((bf16[2048]{0:T(1024)(128)(2,1)S(1)}, bf16[2048]{0:T(1024)(128)(2,1)S(1)}, u32[]{:S(2)}, u32[]{:S(2)}) %collective-permute-start.10) | collective-permute-done | bytes 4128 | tf_op jit(solution)/shard_map/ppermute | solution.py:25
  225.9 2.5 %collective-permute-start.9 = (bf16[2048]{0:T(1024)(128)(2,1)S(1)}, bf16[2048]{0:T(1024)(128)(2,1)S(1)}, u32[]{:S(2)}, u32[]{:S(2)}) collective-permute-start(bf16[2048]{0:T(1024)(128)(2,1)S(1)} %get-tuple-element.315), channel_id=1, source_target_pairs={{0,1},{1,2},{2,3},{3,4},{4,5},{5,6},{6,7},{7,8},{8,9},{9,10},{10,1... | collective-permute-start | bytes 12296 | tf_op jit(solution)/shard_map/ppermute | solution.py:25
  228.4 6.7 %collective-permute-done.9 = bf16[2048]{0:T(1024)(128)(2,1)S(1)} collective-permute-done((bf16[2048]{0:T(1024)(128)(2,1)S(1)}, bf16[2048]{0:T(1024)(128)(2,1)S(1)}, u32[]{:S(2)}, u32[]{:S(2)}) %collective-permute-start.9) | collective-permute-done | bytes 4128 | tf_op jit(solution)/shard_map/ppermute | solution.py:25
  235.1 2.4 %divide_convert_fusion = bf16[2048,128]{1,0:T(8,128)(2,1)} fusion(bf16[2048,128]{1,0:T(8,128)(2,1)S(1)} %collective-permute-done.7, bf16[2048,128]{1,0:T(8,128)(2,1)S(1)} %collective-permute-done.6, bf16[2048,128]{1,0:T(8,128)(2,1)S(1)} %collective-permute-done.5, f32[8192,128]{1,0:T(8,128)} %get-tuple-element.262, f32[2048]{0:T(1024)S(1)} %add_maximum_fusion), kind=kLoop, calls=%fused_computation.146 | loop fusion | flops 2097152 | bytes 3153920 | tf_op jit(solution)/shard_map/convert_element_type | solution.py:156
  (77 shorter events, 31.8 us)
Async XLA Ops:
  0.0 31.0 %copy-start = (f32[4,4096]{1,0:T(4,128)S(1)}, f32[4,4096]{1,0:T(4,128)}, u32[]{:S(2)}) copy-start(f32[4,4096]{1,0:T(4,128)} %param.24) | copy-start | bytes 196612
  0.0 14.4 %copy-start.2 = (bf16[2048,128]{1,0:T(8,128)(2,1)S(1)}, bf16[2048,128]{1,0:T(8,128)(2,1)}, u32[]{:S(2)}) copy-start(bf16[2048,128]{1,0:T(8,128)(2,1)} %param.16) | copy-start | bytes 1572868
  0.0 14.1 %copy-start.5 = (bf16[7,128,128]{2,1,0:T(8,128)(2,1)S(1)}, bf16[7,128,128]{2,1,0:T(8,128)(2,1)}, u32[]{:S(2)}) copy-start(bf16[7,128,128]{2,1,0:T(8,128)(2,1)} %param.17) | copy-start | bytes 688132
  0.8 13.6 %collective-permute-start = (bf16[3,128]{1,0:T(4,128)(2,1)S(1)}, bf16[3,128]{1,0:T(4,128)(2,1)S(1)}, u32[]{:S(2)}, u32[]{:S(2)}) collective-permute-start(bf16[3,128]{1,0:T(4,128)(2,1)S(1)} %get-tuple-element.311), channel_id=1, source_target_pairs={{0,1},{1,2},{2,3},{3,4},{4,5},{5,6},{6,7},{7,8},{8,9},{9,10},{10,1... | collective-permute-start | bytes 2312 | tf_op jit(solution)/shard_map/ppermute | solution.py:14
  2.7 12.3 %copy-start.9 = (f32[128]{0:T(128)S(1)}, f32[128]{0:T(128)}, u32[]{:S(2)}) copy-start(f32[128]{0:T(128)} %param.18) | copy-start | bytes 1540
  2.7 10.3 %collective-permute-start.1 = (bf16[3,128]{1,0:T(4,128)(2,1)S(1)}, bf16[3,128]{1,0:T(4,128)(2,1)S(1)}, u32[]{:S(2)}, u32[]{:S(2)}) collective-permute-start(bf16[3,128]{1,0:T(4,128)(2,1)S(1)} %get-tuple-element.312), channel_id=1, source_target_pairs={{1,0},{2,1},{3,2},{4,3},{5,4},{6,5},{7,6},{8,7},{9,8},{10,9},{11,1... | collective-permute-start | bytes 2312 | tf_op jit(solution)/shard_map/ppermute | solution.py:17
  15.0 12.7 %copy-start.7 = (s32[4]{0:T(128)S(1)}, s32[4]{0:T(128)}, u32[]{:S(2)}) copy-start(s32[4]{0:T(128)} %param.25) | copy-start | bytes 52
  15.0 16.0 %copy-start.10 = (s32[4]{0:T(128)S(1)}, s32[4]{0:T(128)}, u32[]{:S(2)}) copy-start(s32[4]{0:T(128)} %param.26) | copy-start | bytes 52
  16.0 15.9 %collective-permute-start.2 = (bf16[2048,128]{1,0:T(8,128)(2,1)S(1)}, bf16[2048,128]{1,0:T(8,128)(2,1)S(1)}, u32[]{:S(2)}, u32[]{:S(2)}) collective-permute-start(bf16[2048,128]{1,0:T(8,128)(2,1)S(1)} %fusion.118), channel_id=1, source_target_pairs={{0,1},{1,2},{2,3},{3,4},{4,5},{5,6},{6,7},{7,8},{8,9},{9,10},{10,1... | collective-permute-start | bytes 1572872 | tf_op jit(solution)/shard_map/ppermute | solution.py:25
  17.9 18.8 %collective-permute-start.3 = (bf16[2048,128]{1,0:T(8,128)(2,1)S(1)}, bf16[2048,128]{1,0:T(8,128)(2,1)S(1)}, u32[]{:S(2)}, u32[]{:S(2)}) collective-permute-start(bf16[2048,128]{1,0:T(8,128)(2,1)S(1)} %fusion.118), channel_id=1, source_target_pairs={{1,0},{2,1},{3,2},{4,3},{5,4},{6,5},{7,6},{8,7},{9,8},{10,9},{11,1... | collective-permute-start | bytes 1572872 | tf_op jit(solution)/shard_map/ppermute | solution.py:25
  25.8 17.9 %collective-permute-start.4 = (bf16[2048,128]{1,0:T(8,128)(2,1)S(1)}, bf16[2048,128]{1,0:T(8,128)(2,1)S(1)}, u32[]{:S(2)}, u32[]{:S(2)}) collective-permute-start(bf16[2048,128]{1,0:T(8,128)(2,1)S(1)} %fusion.118), channel_id=1, source_target_pairs={{2,0},{3,1},{4,2},{5,3},{6,4},{7,5},{8,6},{9,7},{10,8},{11,9},{12,... | collective-permute-start | bytes 1572872 | tf_op jit(solution)/shard_map/ppermute | solution.py:25
  47.2 2.6 %copy-start.3 = (bf16[3,3,256,256]{3,2,1,0:T(8,128)(2,1)S(1)}, bf16[3,3,256,256]{3,2,1,0:T(8,128)(2,1)}, u32[]{:S(2)}) copy-start(bf16[3,3,256,256]{3,2,1,0:T(8,128)(2,1)} %param.20) | copy-start | bytes 3538948
  47.2 2.6 %copy-start.4 = (bf16[3,128,256]{2,1,0:T(8,128)(2,1)S(1)}, bf16[3,128,256]{2,1,0:T(8,128)(2,1)}, u32[]{:S(2)}) copy-start(bf16[3,128,256]{2,1,0:T(8,128)(2,1)} %param.19) | copy-start | bytes 589828
  47.2 2.6 %copy-start.6 = (f32[4,256]{1,0:T(4,128)S(1)}, f32[4,256]{1,0:T(4,128)}, u32[]{:S(2)}) copy-start(f32[4,256]{1,0:T(4,128)} %param.21) | copy-start | bytes 12292
  47.2 2.6 %copy-start.11 = (f32[128]{0:T(128)S(1)}, f32[128]{0:T(128)}, u32[]{:S(2)}) copy-start(f32[128]{0:T(128)} %param.23) | copy-start | bytes 1540
  76.6 2.2 copy-start.8
  126.0 111.5 %copy-start.1 = (f32[4,4096]{1,0:T(4,128)S(1)}, f32[4,4096]{1,0:T(4,128)}, u32[]{:S(2)}) copy-start(f32[4,4096]{1,0:T(4,128)} %param.24) | copy-start | bytes 196612
  128.5 106.6 %collective-permute-start.5 = (bf16[2048,128]{1,0:T(8,128)(2,1)S(1)}, bf16[2048,128]{1,0:T(8,128)(2,1)S(1)}, u32[]{:S(2)}, u32[]{:S(2)}) collective-permute-start(bf16[2048,128]{1,0:T(8,128)(2,1)S(1)} %get-tuple-element.304), channel_id=1, source_target_pairs={{1,0},{2,1},{3,2},{4,3},{5,4},{6,5},{7,6},{8,7},{9,8},{10,9},{11,1... | collective-permute-start | bytes 1572872 | tf_op jit(solution)/shard_map/ppermute | solution.py:25
  132.7 102.4 %collective-permute-start.6 = (bf16[2048,128]{1,0:T(8,128)(2,1)S(1)}, bf16[2048,128]{1,0:T(8,128)(2,1)S(1)}, u32[]{:S(2)}, u32[]{:S(2)}) collective-permute-start(bf16[2048,128]{1,0:T(8,128)(2,1)S(1)} %get-tuple-element.306), channel_id=1, source_target_pairs={{0,1},{1,2},{2,3},{3,4},{4,5},{5,6},{6,7},{7,8},{8,9},{9,10},{10,1... | collective-permute-start | bytes 1572872 | tf_op jit(solution)/shard_map/ppermute | solution.py:25
  205.7 29.4 %collective-permute-start.7 = (bf16[2048,128]{1,0:T(8,128)(2,1)S(1)}, bf16[2048,128]{1,0:T(8,128)(2,1)S(1)}, u32[]{:S(2)}, u32[]{:S(2)}) collective-permute-start(bf16[2048,128]{1,0:T(8,128)(2,1)S(1)} %get-tuple-element.305), channel_id=1, source_target_pairs={{0,2},{1,3},{2,4},{3,5},{4,6},{5,7},{6,8},{7,9},{8,10},{9,11},{10,... | collective-permute-start | bytes 1572872 | tf_op jit(solution)/shard_map/ppermute | solution.py:25
  209.2 16.7 %collective-permute-start.10 = (bf16[2048]{0:T(1024)(128)(2,1)S(1)}, bf16[2048]{0:T(1024)(128)(2,1)S(1)}, u32[]{:S(2)}, u32[]{:S(2)}) collective-permute-start(bf16[2048]{0:T(1024)(128)(2,1)S(1)} %get-tuple-element.314), channel_id=1, source_target_pairs={{0,2},{1,3},{2,4},{3,5},{4,6},{5,7},{6,8},{7,9},{8,10},{9,11},{10,... | collective-permute-start | bytes 12296 | tf_op jit(solution)/shard_map/ppermute | solution.py:25
  211.4 17.0 %collective-permute-start.8 = (bf16[2048]{0:T(1024)(128)(2,1)S(1)}, bf16[2048]{0:T(1024)(128)(2,1)S(1)}, u32[]{:S(2)}, u32[]{:S(2)}) collective-permute-start(bf16[2048]{0:T(1024)(128)(2,1)S(1)} %get-tuple-element.313), channel_id=1, source_target_pairs={{1,0},{2,1},{3,2},{4,3},{5,4},{6,5},{7,6},{8,7},{9,8},{10,9},{11,1... | collective-permute-start | bytes 12296 | tf_op jit(solution)/shard_map/ppermute | solution.py:25
  225.9 9.1 %collective-permute-start.9 = (bf16[2048]{0:T(1024)(128)(2,1)S(1)}, bf16[2048]{0:T(1024)(128)(2,1)S(1)}, u32[]{:S(2)}, u32[]{:S(2)}) collective-permute-start(bf16[2048]{0:T(1024)(128)(2,1)S(1)} %get-tuple-element.315), channel_id=1, source_target_pairs={{0,1},{1,2},{2,3},{3,4},{4,5},{5,6},{6,7},{7,8},{8,9},{9,10},{10,1... | collective-permute-start | bytes 12296 | tf_op jit(solution)/shard_map/ppermute | solution.py:25
where the time goes:
time: 240 us; the launch traced here: 237 us
  starting transfers between devices  114 us (48%)
  local copies, waits for them, and re-layouts  37.2 us (16%)
  waiting for transfers between devices  25.6 us (11%)
  other arithmetic  25.3 us (11%)
  matrix products  25 us (10%)
  loops' own time  7.34 us (3%)
  between operations  2.93 us (1%)
    ppermute x9, starting transfers between devices, shifted(): return lax.ppermute(block, axis, route)  104 us
    dynamic_update_slice x4, local copies, waits for them, and re-layouts, add_window(): lax.dynamic_update_slice_in_dim(weighted, previous + output.astype(jnp.fl...  25.9 us
    ppermute x9, waiting for transfers between devices, shifted(): return lax.ppermute(block, axis, route)  25.6 us
    dot_general x11, matrix products, temporal_net(): jnp.dot(padded[k * spread:k * spread + length], kernel[k], preferred_elem...  14.6 us
    add x4, other arithmetic, add_window(): previous + output.astype(jnp.float32) * weight_row[:, None]  8.84 us
    ppermute x1, starting transfers between devices, padded_2(): lax.ppermute(lax.slice_in_dim(block, 0, width, axis=dim), axis, backward)  7.86 us
    another operation x1, loops' own time, per_device(): weighted, weight_total = lax.fori_loop(0, slot_count, add_window, initial)  5.54 us
    dot_general x1, matrix products, temporal_net(): jnp.dot(hidden, head_weight, preferred_element_type=jnp.float32) + head_bias  5.3 us
  transfers between devices with their start and end apart: 11, of which 4 were waited for; matrix products, arithmetic and copies ran while one was open for 2% of the time, Pallas kernels for 0%

commit v1 on v0

v1 whole, which is shorter than its diff:
```python
import functools
import math

import jax
import jax.numpy as jnp
from jax import lax
from jax.experimental import pallas as pl
from jax.experimental.pallas import tpu as pltpu
from jax.sharding import PartitionSpec as P

bf16, f32, i32 = jnp.bfloat16, jnp.float32, jnp.int32
MESH = pl.DeviceIdType.MESH
EPS = 1e-05
SEG = 256
HALO = 32
WSEG = 16
SHARD = 2048
NSEG = SHARD // SEG
SLOTS = 16
DEAD = -100000
G1 = math.sqrt(2.0 / math.pi)
G2 = G1 * 0.044715


def gelu32(v):
    half = 0.5 * v
    return half + half * jnp.tanh(v * (G1 + G2 * (v * v)))


def gelu16(v):
    v = v.astype(bf16)
    half = bf16(0.5) * v
    return half + half * jnp.tanh(v * (bf16(G1) + bf16(G2) * (v * v)))


def feature_kernel(
    count, table, stream, weight, bias, feats, norms, rows, stats, local_sem, halo_send, halo_recv,
    stat_send, stat_recv,
):
    me = lax.axis_index("tm")

    def at(offset):
        return lax.rem(me + offset + count, count)

    load = pltpu.make_async_copy(stream, rows.at[pl.ds(48, SHARD)], local_sem)
    load.start()
    barrier = pltpu.get_barrier_semaphore()
    for offset in (-2, -1, 1, 2):
        pl.semaphore_signal(barrier, inc=1, device_id=(at(offset),), device_id_type=MESH)
    pl.semaphore_wait(barrier, 4)
    to_right = pltpu.make_async_remote_copy(
        src_ref=stream.at[pl.ds(SHARD - 48, 48)], dst_ref=rows.at[pl.ds(0, 48)],
        send_sem=halo_send.at[0], recv_sem=halo_recv.at[0], device_id=(at(1),), device_id_type=MESH,
    )
    to_left = pltpu.make_async_remote_copy(
        src_ref=stream.at[pl.ds(0, 16)], dst_ref=rows.at[pl.ds(SHARD + 48, 16)],
        send_sem=halo_send.at[1], recv_sem=halo_recv.at[1], device_id=(at(-1),), device_id_type=MESH,
    )
    to_right.start()
    to_left.start()
    load.wait()

    def stem(first, length):
        block = rows[pl.ds(first + 32, length + 32)]
        wide = jnp.concatenate([block[13 + k : 13 + k + length] for k in range(7)], axis=1)
        summed = jnp.dot(wide, weight[...], preferred_element_type=f32) + bias[...]
        made = gelu32(summed).astype(bf16)
        feats[pl.ds(first + HALO, length)] = made
        return made.astype(f32)

    def tile(index):
        made = stem(index * 512, 512)
        for half in range(2):
            part = made[half * SEG : (half + 1) * SEG]
            row = 16 + index * 2 + half
            stats[0, row : row + 1] = jnp.sum(part, axis=0, keepdims=True)
            stats[1, row : row + 1] = jnp.sum(part * part, axis=0, keepdims=True)

    tile(1)
    tile(2)
    to_right.wait()
    to_left.wait()

    @pl.when(me == 0)
    def _():
        rows[pl.ds(0, 48)] = jnp.zeros((48, 128), bf16)

    @pl.when(me == count - 1)
    def _():
        rows[pl.ds(SHARD + 48, 16)] = jnp.zeros((16, 128), bf16)

    tile(3)
    tile(0)
    copies = []
    for index, offset in enumerate((-2, -1, 1, 2)):
        copies.append(
            pltpu.make_async_remote_copy(
                src_ref=stats.at[:, pl.ds(16, 8)], dst_ref=stats.at[:, pl.ds(8 * (2 - offset), 8)],
                send_sem=stat_send.at[index], recv_sem=stat_recv.at[index],
                device_id=(at(offset),), device_id_type=MESH,
            )
        )
    for copy in copies:
        copy.start()
    stem(-HALO, HALO)
    for copy in copies:
        copy.wait()
    for slot in range(SLOTS):
        owner = me + slot // 4 - 2
        inside = jnp.logical_and(owner >= 0, owner < count)
        start = jnp.where(inside, table[jnp.clip(owner, 0, count - 1) * 8 + slot % 4], 0)
        first = jnp.clip(start - NSEG * me + 16, 0, 24)
        row = lax.broadcasted_iota(i32, (40, 128), 0)
        covered = jnp.logical_and(row >= first, row < first + WSEG)
        mean, square = (
            jnp.sum(jnp.where(covered, stats[n], 0.0), axis=0, keepdims=True) * (1.0 / (WSEG * SEG))
            for n in range(2)
        )
        scale = lax.rsqrt(square - mean * mean + EPS)
        norms[slot : slot + 1] = scale
        norms[SLOTS + slot : SLOTS + slot + 1] = -mean * scale


def make_features(count, table, stream, weight, bias):
    return pl.pallas_call(
        functools.partial(feature_kernel, count),
        out_shape=[
            jax.ShapeDtypeStruct((SHARD + HALO, 128), bf16),
            jax.ShapeDtypeStruct((2 * SLOTS, 128), f32),
        ],
        in_specs=[
            pl.BlockSpec(memory_space=pltpu.SMEM),
            pl.BlockSpec(memory_space=pl.ANY),
            pl.BlockSpec(memory_space=pltpu.VMEM),
            pl.BlockSpec(memory_space=pltpu.VMEM),
        ],
        out_specs=[pl.BlockSpec(memory_space=pltpu.VMEM)] * 2,
        scratch_shapes=[
            pltpu.VMEM((SHARD + 64, 128), bf16),
            pltpu.VMEM((2, 40, 128), f32),
            pltpu.SemaphoreType.DMA,
            pltpu.SemaphoreType.DMA((2,)),
            pltpu.SemaphoreType.DMA((2,)),
            pltpu.SemaphoreType.DMA((4,)),
            pltpu.SemaphoreType.DMA((4,)),
        ],
        compiler_params=pltpu.CompilerParams(
            collective_id=0, has_side_effects=True, vmem_limit_bytes=24 * 2**20
        ),
    )(table, stream, weight, bias)


BIG, SMALL = 2048, 512
CAPACITY = 128 * SEG + 64 * HALO + BIG
UNITS = 160


def network_kernel(
    count, table, feats, norms, first_weight, deep_weight, layer_bias, head_weight, head_bias,
    profiles, out, x_stack, h_a, h_b, total, columns, padded, weights, unit, zeros,
):
    me = lax.axis_index("tm")

    padded[...] = jnp.zeros_like(padded)
    for p in range(4):
        for k in range(WSEG):
            padded[p * 32 + 8 + k : p * 32 + 9 + k] = profiles[p : p + 1, k * SEG : (k + 1) * SEG]
    for block in range(32):
        part = profiles[:, block * 128 : (block + 1) * 128]
        part = jnp.concatenate([part, jnp.zeros((4, 128), f32)], axis=0)
        columns[block * 128 : (block + 1) * 128] = part.T
    weights[...] = jnp.zeros_like(weights)

    def clear(index, carry):
        total[pl.ds(pl.multiple_of(index * SEG, SEG), SEG)] = jnp.zeros((SEG, 128), f32)
        return carry

    lax.fori_loop(0, NSEG, clear, 0)

    def own_slot(slot, state):
        owner = me + slot // 4 - 2
        inside = jnp.logical_and(owner >= 0, owner < count)
        place = jnp.clip(owner, 0, count - 1) * 8 + lax.rem(slot, 4)
        start = jnp.where(inside, table[place], DEAD)
        profile = table[place + 4]
        rel = start - NSEG * me
        low, high = jnp.maximum(rel, 0), jnp.minimum(rel + WSEG, NSEG)
        scale = norms[pl.ds(slot, 1)]
        shift = norms[pl.ds(SLOTS + slot, 1)]

        def normalised(row, length):
            block = feats[pl.ds(pl.multiple_of(row, 32), length)].astype(f32)
            return (block * scale + shift).astype(bf16)

        def begin(state):
            rows, units, blanks = state
            rows = pl.multiple_of(rows, 32)
            for k in range(NSEG):
                weights[k : k + 1] += padded[pl.ds(profile * 32 + 8 - rel + k, 1)]

            @pl.when(rel >= 0)
            def _():
                x_stack[pl.ds(rows + HALO, HALO)] = jnp.zeros((HALO, 128), bf16)
                zeros[blanks] = rows + HALO

            @pl.when(rel < 0)
            def _():
                x_stack[pl.ds(rows + HALO, HALO)] = normalised(low * SEG, HALO)

            return rows + HALO, units, blanks + jnp.where(rel >= 0, 1, 0)

        def segment(k, state):
            rows, units, blanks = state
            rows = pl.multiple_of(rows, 32)
            x_stack[pl.ds(rows + HALO, SEG)] = normalised(k * SEG + HALO, SEG)
            unit[0, units] = rows
            unit[1, units] = k
            unit[2, units] = (k - rel) * SEG
            unit[3, units] = profile
            return rows + SEG, units + 1, blanks

        state = lax.cond(high > low, begin, lambda s: s, state)
        return lax.fori_loop(low, high, segment, state)

    rows, units, blanks = lax.fori_loop(0, SLOTS, own_slot, (i32(0), i32(0), i32(0)))

    big = rows // BIG
    left = rows - big * BIG
    small = (left + SMALL - 1) // SMALL

    def over_rows(body):
        def big_step(index, carry):
            body(pl.multiple_of(index * BIG, BIG), BIG)
            return carry

        def small_step(index, carry):
            body(pl.multiple_of(big * BIG + index * SMALL, SMALL), SMALL)
            return carry

        lax.fori_loop(0, big, big_step, 0)
        lax.fori_loop(0, small, small_step, 0)

    def layer(index, source, target, weight):
        spread = 2**index

        def body(first, length):
            block = source[pl.ds(first, length + HALO)]
            wide = jnp.concatenate(
                [block[HALO - s * spread : HALO - s * spread + length] for s in (2, 1, 0)], axis=1
            )
            summed = jnp.dot(wide, weight, preferred_element_type=f32)
            made = gelu16(summed + layer_bias[index : index + 1])
            if index:
                made = made + block[HALO:]
            target[pl.ds(first + HALO, length)] = made

        over_rows(body)

        def blank(n, carry):
            target[pl.ds(pl.multiple_of(zeros[n], 32), HALO)] = jnp.zeros((HALO, 256), bf16)
            return carry

        lax.fori_loop(0, blanks, blank, 0)

    layer(0, x_stack, h_a, first_weight[...])
    layer(1, h_a, h_b, deep_weight[0])
    layer(2, h_b, h_a, deep_weight[1])
    layer(3, h_a, h_b, deep_weight[2])

    def head(first, length):
        made = jnp.dot(
            h_b[pl.ds(first + HALO, length)], head_weight[...], preferred_element_type=f32
        )
        x_stack[pl.ds(first + HALO, length)] = (made + head_bias[...]).astype(bf16)

    over_rows(head)

    def gather(n, carry):
        rows = pl.multiple_of(unit[0, n] + HALO, 32)
        target = pl.ds(pl.multiple_of(unit[1, n] * SEG, SEG), SEG)
        offset = pl.ds(pl.multiple_of(unit[2, n], SEG), SEG)
        for p in range(4):

            @pl.when(unit[3, n] == p)
            def _():
                made = x_stack[pl.ds(rows, SEG)].astype(f32)
                total[target] += made * columns[offset, p : p + 1]

        return carry

    lax.fori_loop(0, units, gather, 0)

    inverse = 1.0 / jnp.maximum(weights[...], 1.0)
    for half in range(2):
        column = inverse[:, half * 128 : (half + 1) * 128].T
        for k in range(NSEG):
            where = pl.ds(k * SEG + half * 128, 128)
            out[where] = (total[where] * column[:, k : k + 1]).astype(bf16)


def run_network(count, table, feats, norms, net, profiles):
    vmem = pl.BlockSpec(memory_space=pltpu.VMEM)
    return pl.pallas_call(
        functools.partial(network_kernel, count),
        out_shape=jax.ShapeDtypeStruct((SHARD, 128), bf16),
        in_specs=[pl.BlockSpec(memory_space=pltpu.SMEM)] + [vmem] * 8,
        out_specs=vmem,
        scratch_shapes=[
            pltpu.VMEM((CAPACITY + HALO, 128), bf16),
            pltpu.VMEM((CAPACITY + HALO, 256), bf16),
            pltpu.VMEM((CAPACITY + HALO, 256), bf16),
            pltpu.VMEM((SHARD, 128), f32),
            pltpu.VMEM((4096, 8), f32),
            pltpu.VMEM((4 * 32, SEG), f32),
            pltpu.VMEM((NSEG, SEG), f32),
            pltpu.SMEM((4, UNITS), i32),
            pltpu.SMEM((UNITS,), i32),
        ],
        compiler_params=pltpu.CompilerParams(vmem_limit_bytes=60 * 2**20),
    )(table, feats, norms, *net, profiles)


def per_device(
    stream, stem_weight, stem_bias, first_weight, deep_weight, layer_bias, head_weight, head_bias,
    profiles, starts, profile_index, counts,
):
    count = lax.axis_size("tm")
    live = jnp.arange(4, dtype=i32) < counts[0]
    mine = jnp.concatenate([jnp.where(live, starts // SEG, DEAD), profile_index])
    table = lax.all_gather(mine, "tm", tiled=True)
    feats, norms = make_features(
        count, table, stream, stem_weight.reshape(7 * 128, 128), stem_bias.reshape(1, 128)
    )
    net = (
        first_weight.reshape(3 * 128, 256),
        deep_weight.reshape(3, 3 * 256, 256),
        layer_bias,
        head_weight,
        head_bias.reshape(1, 128),
    )
    return run_network(count, table, feats, norms, net, profiles)


def solution(mesh):
    in_specs = (P("tm", None), P(), P(), P(), P(), P(), P(), P(), P(), P("tm"), P("tm"), P("tm"))
    return jax.shard_map(
        per_device, mesh=mesh, in_specs=in_specs, out_specs=P("tm", None), check_vma=False
    )
```

time: 240 us -> 146 us (0.61)
  the two profiles are of different devices: /device:TPU:24 before, /device:TPU:107 now
where the time goes in v1:
time: 146 us; the launch traced here: 145 us
  Pallas kernels  75.9 us (52%)
  blocking collectives  63.1 us (43%)
  local copies, waits for them, and re-layouts  4.03 us (3%)
  other arithmetic  1.51 us (1%)
    pallas_call x1, Pallas kernels, run_network(): pl.pallas_call(functools.partial(network_kernel, count), out_shape=jax.Sh...  65.8 us
    unnamed x1, blocking collectives  63.1 us
    pallas_call x1, Pallas kernels, make_features(): pl.pallas_call(functools.partial(feature_kernel, count), out_shape=[jax.S...  10.1 us
    unnamed x13, local copies, waits for them, and re-layouts  4.03 us

profile of v1, /device:TPU:107, one launch (start us, length us, event | category | flops | bytes accessed | tf_op | source)
XLA Modules:
  0.0 145.2 jit_solution(382374420292430712)
XLA Ops:
  0.7 0.7 compare_select_fusion
  1.3 0.8 add_dynamic-update-slice_fusion
  2.2 63.1 %all-reduce.table = s32[1024]{0:T(1024)S(1)} all-reduce(s32[1024]{0:T(1024)S(1)} %add_dynamic-update-slice_fusion), channel_id=1, replica_groups=mesh['tm'=128] {'tm'}, use_global_device_ids=true, to_apply=%add | all-reduce | flops 1024 | bytes 8192
  65.3 0.0 copy-start.1
  65.3 1.0 copy-done.1
  66.3 0.0 copy-start.2
  66.3 0.9 copy-done.2
  67.3 0.0 copy-start.5
  67.3 0.7 copy-done.5
  67.9 0.0 copy-start.3
  67.9 10.1 %shard_map.118 = (bf16[2080,128]{1,0:T(8,128)(2,1)S(1)}, f32[32,128]{1,0:T(8,128)S(1)}) custom-call(s32[1024]{0:T(1024)S(1)} %all-reduce.table, bf16[2048,128]{1,0:T(8,128)(2,1)S(1)} %copy-done.1, bf16[896,128]{1,0:T(8,128)(2,1)S(1)} %bitcast.7, f32[1,128]{1,0:T(1,128)S(1)} %bitcast.8), custom_call_target="tpu_custom_call" | custom-call | tf_op jit(solution)/shard_map/pallas_call | solution.py:125
  78.0 0.0 copy-start
  78.0 0.8 copy-done
  78.8 0.0 copy-start.4
  78.8 0.6 copy-done.4
  79.4 0.0 copy-done.3
  79.4 65.8 %shard_map.119 = bf16[2048,128]{1,0:T(8,128)(2,1)} custom-call(s32[1024]{0:T(1024)} %copy-done.3, bf16[2080,128]{1,0:T(8,128)(2,1)} %copy-done, f32[32,128]{1,0:T(8,128)} %copy-done.4, bf16[384,256]{1,0:T(8,128)(2,1)} %bitcast.10, bf16[3,768,256]{2,1,0:T(8,128)(2,1)} %bitcast.9, f32[4,256]{1,0:T(4,128)} %layer_bias.1, bf16[256,128]{1,0:T(8,128)(2,1)} %head_weight.1, ...), custom_call_target="tpu_custom_call" | custom-call | tf_op jit(solution)/shard_map/pallas_call | solution.py:303
  (1 shorter events, 0.0 us)
Async XLA Ops:
  65.3 1.0 copy-start.1
  66.3 0.9 copy-start.2
  67.3 0.7 copy-start.5
  67.9 11.5 %copy-start.3 = (s32[1024]{0:T(1024)}, s32[1024]{0:T(1024)S(1)}, u32[]{:S(2)}) copy-start(s32[1024]{0:T(1024)S(1)} %all-reduce.table) | copy-start | bytes 12292
  78.0 0.8 copy-start
  78.8 0.6 copy-start.4

commit v2 on v1

v2 whole, which is shorter than its diff:
```python
import functools
import math

import jax
import jax.numpy as jnp
from jax import lax
from jax.experimental import pallas as pl
from jax.experimental.pallas import tpu as pltpu
from jax.sharding import PartitionSpec as P

bf16, f32, i32 = jnp.bfloat16, jnp.float32, jnp.int32
MESH = pl.DeviceIdType.MESH
EPS = 1e-05
SEG = 256
HALO = 32
WSEG = 16
SHARD = 2048
NSEG = SHARD // SEG
SLOTS = 16
DEAD = -100000
G1 = math.sqrt(2.0 / math.pi)
G2 = G1 * 0.044715


def gelu32(v):
    half = 0.5 * v
    return half + half * jnp.tanh(v * (G1 + G2 * (v * v)))


def gelu16(v):
    v = v.astype(bf16)
    half = bf16(0.5) * v
    return half + half * jnp.tanh(v * (bf16(G1) + bf16(G2) * (v * v)))


def other_core(d):
    return d + 1 - 2 * (d % 2)


def along_y(d, step):
    return (d + 32 * step + 128) % 128


def along_z(d, step):
    return d // 32 * 32 + (d % 32 + 8 * step + 32) % 32


def along_x(d, step):
    return d // 8 * 8 + (d % 8 + 2 * step + 8) % 8


def helper(d, k):
    if k == 0:
        return other_core(along_y(d, 1))
    if k == 1:
        return along_y(d, -1)
    if k == 2:
        return other_core(along_z(d, 1))
    return along_z(d, -1)


def helped(d, k):
    if k == 0:
        return along_y(other_core(d), -1)
    if k == 1:
        return along_y(d, 1)
    if k == 2:
        return along_z(other_core(d), -1)
    return along_z(d, 1)


def lanes_core(v, lane):
    return jnp.where(lane % 2 == 0, pltpu.roll(v, 127, 1), pltpu.roll(v, 1, 1))


def lanes_y(v, lane, step):
    return pltpu.roll(v, 96 if step > 0 else 32, 1)


def lanes_z(v, lane, step):
    if step > 0:
        return jnp.where(lane % 32 < 24, pltpu.roll(v, 120, 1), pltpu.roll(v, 24, 1))
    return jnp.where(lane % 32 >= 8, pltpu.roll(v, 8, 1), pltpu.roll(v, 104, 1))


def at_helper(v, lane, k):
    if k == 0:
        return lanes_y(lanes_core(v, lane), lane, 1)
    if k == 1:
        return lanes_y(v, lane, -1)
    if k == 2:
        return lanes_z(lanes_core(v, lane), lane, 1)
    return lanes_z(v, lane, -1)


def at_helped(v, lane, k):
    if k == 0:
        return lanes_core(lanes_y(v, lane, -1), lane)
    if k == 1:
        return lanes_y(v, lane, 1)
    if k == 2:
        return lanes_core(lanes_z(v, lane, -1), lane)
    return lanes_z(v, lane, 1)


def share_out(rows):
    lane = lax.broadcasted_iota(i32, (8, 128), 1)
    segment = (lane * NSEG + lax.broadcasted_iota(i32, (8, 128), 0)).astype(f32)
    covering = jnp.zeros((8, 128), f32)
    for j in range(4):
        start = jnp.broadcast_to(rows[j : j + 1], (8, 128))
        for offset in range(-2, 2):
            moved = pltpu.roll(start, (-offset) % 128, 1) if offset else start
            there = jnp.logical_and(lane + offset >= 0, lane + offset < 128)
            there = jnp.logical_and(there, jnp.logical_and(segment >= moved, segment < moved + WSEG))
            covering = covering + jnp.where(there, 1.0, 0.0)
    caps = [
        jnp.broadcast_to(covering[2 * k : 2 * k + 1] + covering[2 * k + 1 : 2 * k + 2], (8, 128))
        for k in range(4)
    ]
    load = caps[0] + caps[1] + caps[2] + caps[3]
    given = [jnp.zeros((8, 128), f32) for _ in range(4)]
    for _ in range(4):
        for k in range(4):
            half = 0.5 * (load - at_helper(load, lane, k))
            move = jnp.where(half >= 0, jnp.floor(half), -jnp.floor(-half))
            move = jnp.clip(move, -given[k], caps[k] - given[k])
            given[k] = given[k] + move
            load = load - move + at_helped(move, lane, k)
    return given


def feature_kernel(
    count, starts, profile_index, live, stream, weight_hbm, bias, feats, norms, table, shares, lent, lent_norms,
    rows, weight, stats, known, local_sem, halo_send, halo_recv, stat_send, stat_recv, known_send, known_recv,
    lent_send, lent_recv, norm_send, norm_recv,
):
    me = lax.axis_index("tm")

    def at(offset):
        return lax.rem(me + offset + count, count)

    load = pltpu.make_async_copy(stream, rows.at[pl.ds(48, SHARD)], local_sem.at[0])
    load.start()
    load_weight = pltpu.make_async_copy(weight_hbm, weight, local_sem.at[1])
    load_weight.start()

    lane = lax.broadcasted_iota(i32, (1, 128), 1)
    line = jnp.zeros((1, 128), f32)
    for j in range(4):
        start = jnp.where(j < live[0], starts[j] // SEG, DEAD).astype(f32)
        line = jnp.where(lane == j, start, line)
        line = jnp.where(lane == 4 + j, profile_index[j].astype(f32), line)
    known[me] = line

    barrier = pltpu.get_barrier_semaphore()
    partners = [at(offset) for offset in (-2, -1, 1, 2)] + [other_core(me)]
    for step in (1, 2, 3):
        partners += [along_x(me, step), along_y(me, step), along_z(me, step)]
    for k in range(4):
        partners += [helper(me, k), helped(me, k)]
    for partner in partners:
        pl.semaphore_signal(barrier, inc=1, device_id=(partner,), device_id_type=MESH)
    pl.semaphore_wait(barrier, len(partners))

    def send(src, dst, send_sem, recv_sem, device):
        copy = pltpu.make_async_remote_copy(
            src_ref=src, dst_ref=dst, send_sem=send_sem, recv_sem=recv_sem, device_id=(device,),
            device_id_type=MESH,
        )
        copy.start()
        return copy

    def tell(first, length, index, device):
        block = known.at[pl.ds(first, length)]
        return send(block, block, known_send.at[index], known_recv.at[index], device)

    halos = [
        send(stream.at[pl.ds(SHARD - 48, 48)], rows.at[pl.ds(0, 48)], halo_send.at[0], halo_recv.at[0], at(1)),
        send(stream.at[pl.ds(0, 16)], rows.at[pl.ds(SHARD + 48, 16)], halo_send.at[1], halo_recv.at[1], at(-1)),
    ]
    round_c = tell(me, 1, 0, other_core(me))
    load.wait()
    load_weight.wait()

    def stem(first, length):
        block = rows[pl.ds(first + 32, length + 32)]
        wide = jnp.concatenate([block[13 + k : 13 + k + length] for k in range(7)], axis=1)
        summed = jnp.dot(wide, weight[...], preferred_element_type=f32) + bias[...]
        made = gelu32(summed).astype(bf16)
        feats[pl.ds(first + HALO, length)] = made
        return made.astype(f32)

    def tile(index):
        made = stem(index * 512, 512)
        for half in range(2):
            part = made[half * SEG : (half + 1) * SEG]
            row = 16 + index * 2 + half
            stats[0, row : row + 1] = jnp.sum(part, axis=0, keepdims=True)
            stats[1, row : row + 1] = jnp.sum(part * part, axis=0, keepdims=True)

    def lend(k):
        return send(
            feats.at[pl.ds(512 * k, 512 + HALO)], lent.at[k], lent_send.at[k], lent_recv.at[k], helper(me, k)
        )

    tile(1)
    round_c.wait()
    round_x = [tell(me // 2 * 2, 2, step, along_x(me, step)) for step in (1, 2, 3)]
    tile(2)
    loans = [lend(2)]
    for copy in round_x:
        copy.wait()
    round_z = [tell(me // 8 * 8, 8, 3 + step, along_z(me, step)) for step in (1, 2, 3)]
    for copy in halos:
        copy.wait()

    @pl.when(me == 0)
    def _():
        rows[pl.ds(0, 48)] = jnp.zeros((48, 128), bf16)

    @pl.when(me == count - 1)
    def _():
        rows[pl.ds(SHARD + 48, 16)] = jnp.zeros((16, 128), bf16)

    tile(3)
    loans.append(lend(3))
    for copy in round_z:
        copy.wait()
    round_y = [tell(me // 32 * 32, 32, 6 + step, along_y(me, step)) for step in (1, 2, 3)]
    tile(0)
    moments = [
        send(
            stats.at[:, pl.ds(16, 8)], stats.at[:, pl.ds(8 * (2 - offset), 8)], stat_send.at[index],
            stat_recv.at[index], at(offset),
        )
        for index, offset in enumerate((-2, -1, 1, 2))
    ]
    loans.append(lend(1))
    stem(-HALO, HALO)
    loans.append(lend(0))
    for copy in round_y:
        copy.wait()
    for copy in moments:
        copy.wait()

    row = lax.broadcasted_iota(i32, (40, 128), 0).astype(f32)
    for slot in range(SLOTS):
        owner = jnp.clip(me + slot // 4 - 2, 0, count - 1)
        start = known[owner][:, slot % 4 : slot % 4 + 1]
        first = start - (NSEG * me - 16).astype(f32)
        covered = jnp.logical_and(row >= first, row < first + WSEG)
        mean, square = (
            jnp.sum(jnp.where(covered, stats[n], 0.0), axis=0, keepdims=True) * (1.0 / (WSEG * SEG))
            for n in range(2)
        )
        scale = lax.rsqrt(square - mean * mean + EPS)
        norms[slot : slot + 1] = scale
        norms[SLOTS + slot : SLOTS + slot + 1] = -mean * scale
    for k in range(4):
        loans.append(send(norms, lent_norms.at[k], norm_send.at[k], norm_recv.at[k], helper(me, k)))

    turned = known[...].reshape(128, 128).T[:8]
    table[...] = turned.astype(i32)
    given = share_out(turned)
    shares[...] = jnp.concatenate([given[k][:1] for k in range(4)] + [jnp.zeros((4, 128), f32)], axis=0).astype(i32)
    for copy in loans:
        copy.wait()


def make_features(count, starts, profile_index, counts, stream, weight, bias):
    vmem, smem, hbm = (pl.BlockSpec(memory_space=m) for m in (pltpu.VMEM, pltpu.SMEM, pl.ANY))
    dma = pltpu.SemaphoreType.DMA
    return pl.pallas_call(
        functools.partial(feature_kernel, count),
        out_shape=[
            jax.ShapeDtypeStruct((SHARD + HALO, 128), bf16),
            jax.ShapeDtypeStruct((2 * SLOTS, 128), f32),
            jax.ShapeDtypeStruct((8, 128), i32),
            jax.ShapeDtypeStruct((8, 128), i32),
            jax.ShapeDtypeStruct((4, 512 + HALO, 128), bf16),
            jax.ShapeDtypeStruct((4, 2 * SLOTS, 128), f32),
        ],
        in_specs=[smem, smem, smem, hbm, hbm, vmem],
        out_specs=[vmem, vmem, vmem, vmem, hbm, hbm],
        scratch_shapes=[
            pltpu.VMEM((SHARD + 64, 128), bf16),
            pltpu.VMEM((7 * 128, 128), bf16),
            pltpu.VMEM((2, 40, 128), f32),
            pltpu.VMEM((128, 1, 128), f32),
            dma((2,)),
            dma((2,)), dma((2,)),
            dma((4,)), dma((4,)),
            dma((10,)), dma((10,)),
            dma((4,)), dma((4,)),
            dma((4,)), dma((4,)),
        ],
        compiler_params=pltpu.CompilerParams(
            collective_id=0, has_side_effects=True, vmem_limit_bytes=56 * 2**20
        ),
    )(starts, profile_index, counts, stream, weight, bias)


BIG, SMALL = 2048, 512
CAPACITY = 128 * SEG + 128 * HALO + BIG
UNITS = 160


def network_kernel(
    count, table, shares, feats_hbm, lent_hbm, norms_hbm, lent_norms_hbm, first_hbm, deep_hbm, layer_bias, head_hbm,
    head_bias, profiles, sums, weights, lent_sums, feats, norms, first_weight, deep_weight, head_weight, x_stack, h_a,
    h_b, total, columns, padded, unit, zeros, sems,
):
    me = lax.axis_index("tm")
    pieces = [
        (feats_hbm, feats.at[pl.ds(0, SHARD + HALO)]),
        (norms_hbm, norms.at[pl.ds(0, 2 * SLOTS)]),
        (first_hbm, first_weight),
        (deep_hbm, deep_weight),
        (head_hbm, head_weight),
    ]
    for k in range(4):
        pieces.append((lent_hbm.at[k], feats.at[pl.ds(SHARD + HALO + (512 + HALO) * k, 512 + HALO)]))
        pieces.append((lent_norms_hbm.at[k], norms.at[pl.ds(2 * SLOTS * (k + 1), 2 * SLOTS)]))
    loads = [pltpu.make_async_copy(src, dst, sems.at[n]) for n, (src, dst) in enumerate(pieces)]
    for copy in loads:
        copy.start()

    padded[...] = jnp.zeros_like(padded)
    for p in range(4):
        for k in range(WSEG):
            padded[p * 32 + 8 + k : p * 32 + 9 + k] = profiles[p : p + 1, k * SEG : (k + 1) * SEG]
    for block in range(32):
        part = profiles[:, block * 128 : (block + 1) * 128]
        part = jnp.concatenate([part, jnp.zeros((4, 128), f32)], axis=0)
        columns[block * 128 : (block + 1) * 128] = part.T
    weights[...] = jnp.zeros_like(weights)

    def clear(index, carry):
        total[pl.ds(pl.multiple_of(index * SEG, SEG), SEG)] = jnp.zeros((SEG, 128), f32)
        return carry

    lax.fori_loop(0, 2 * NSEG, clear, 0)
    for copy in loads:
        copy.wait()

    def window(home, slot):
        owner = home + slot // 4 - 2
        inside = jnp.logical_and(owner >= 0, owner < count)
        owner = jnp.clip(owner, 0, count - 1)
        start = jnp.where(inside, table[lax.rem(slot, 4), owner], DEAD)
        return start - NSEG * home, table[4 + lax.rem(slot, 4), owner]

    def put(base, target, norm, slot, rel, profile, low, high, fresh, state):
        scale = norms[pl.ds(norm + slot, 1)]
        shift = norms[pl.ds(norm + SLOTS + slot, 1)]

        def normalised(row, length):
            block = feats[pl.ds(pl.multiple_of(row, 32), length)].astype(f32)
            return (block * scale + shift).astype(bf16)

        def begin(state):
            rows, units, blanks = state
            rows = pl.multiple_of(rows, 32)

            @pl.when(low == rel)
            def _():
                x_stack[pl.ds(rows + HALO, HALO)] = jnp.zeros((HALO, 128), bf16)
                zeros[blanks] = rows + HALO

            @pl.when(low != rel)
            def _():
                x_stack[pl.ds(rows + HALO, HALO)] = normalised(base + low * SEG, HALO)

            return rows + HALO, units, blanks + jnp.where(low == rel, 1, 0)

        def segment(k, state):
            rows, units, blanks = state
            rows = pl.multiple_of(rows, 32)
            x_stack[pl.ds(rows + HALO, SEG)] = normalised(base + k * SEG + HALO, SEG)
            unit[0, units] = rows
            unit[1, units] = target + k * SEG
            unit[2, units] = (k - rel) * SEG
            unit[3, units] = profile
            return rows + SEG, units + 1, blanks

        state = lax.cond(fresh, begin, lambda s: s, state)
        return lax.fori_loop(low, high, segment, state)

    def own_slot(slot, carry):
        rel, profile = window(me, slot)

        def covered(carry):
            for k in range(NSEG):
                weights[k : k + 1] += padded[pl.ds(profile * 32 + 8 - rel + k, 1)]
            state, lefts = carry[:3], list(carry[3:])
            end = i32(-1)
            for k in range(4):
                first = jnp.maximum(rel, 2 * k)
                high = jnp.minimum(rel + WSEG, 2 * k + 2)
                given = jnp.minimum(lefts[k], jnp.maximum(high - first, 0))
                lefts[k] = lefts[k] - given
                low = first + given
                fresh = jnp.logical_and(high > low, low != end)
                state = put(0, 0, 0, slot, rel, profile, low, high, fresh, state)
                end = jnp.where(high > low, high, end)
            return (*state, *lefts)

        return lax.cond(jnp.logical_and(rel > -WSEG, rel < NSEG), covered, lambda c: c, carry)

    carry = lax.fori_loop(0, SLOTS, own_slot, (i32(0), i32(0), i32(0), *(shares[k, me] for k in range(4))))
    state = carry[:3]
    for k in range(4):
        home = helped(me, k)
        share = shares[k, home]

        def lent_slot(slot, carry, k=k, home=home):
            rel, profile = window(home, slot)
            first = jnp.maximum(rel, 2 * k)
            taken = jnp.minimum(carry[3], jnp.maximum(jnp.minimum(rel + WSEG, 2 * k + 2) - first, 0))
            state = put(
                SHARD + HALO + HALO * k, SHARD, 2 * SLOTS * (k + 1), slot, rel, profile, first, first + taken,
                taken > 0, carry[:3],
            )
            return (*state, carry[3] - taken)

        state = lax.fori_loop(0, jnp.where(share > 0, SLOTS, 0), lent_slot, (*state, share))[:3]
    rows, units, blanks = state

    big = rows // BIG
    left = rows - big * BIG
    small = (left + SMALL - 1) // SMALL

    def over_rows(body):
        def big_step(index, carry):
            body(pl.multiple_of(index * BIG, BIG), BIG)
            return carry

        def small_step(index, carry):
            body(pl.multiple_of(big * BIG + index * SMALL, SMALL), SMALL)
            return carry

        lax.fori_loop(0, big, big_step, 0)
        lax.fori_loop(0, small, small_step, 0)

    def layer(index, source, target, weight):
        spread = 2**index

        def body(first, length):
            block = source[pl.ds(first, length + HALO)]
            wide = jnp.concatenate(
                [block[HALO - s * spread : HALO - s * spread + length] for s in (2, 1, 0)], axis=1
            )
            summed = jnp.dot(wide, weight, preferred_element_type=f32)
            made = gelu16(summed + layer_bias[index : index + 1])
            if index:
                made = made + block[HALO:]
            target[pl.ds(first + HALO, length)] = made

        over_rows(body)

        def blank(n, carry):
            target[pl.ds(pl.multiple_of(zeros[n], 32), HALO)] = jnp.zeros((HALO, 256), bf16)
            return carry

        lax.fori_loop(0, blanks, blank, 0)

    layer(0, x_stack, h_a, first_weight[...])
    layer(1, h_a, h_b, deep_weight[0])
    layer(2, h_b, h_a, deep_weight[1])
    layer(3, h_a, h_b, deep_weight[2])

    def head(first, length):
        made = jnp.dot(
            h_b[pl.ds(first + HALO, length)], head_weight[...], preferred_element_type=f32
        )
        x_stack[pl.ds(first + HALO, length)] = (made + head_bias[...]).astype(bf16)

    over_rows(head)

    def gather(n, carry):
        rows = pl.multiple_of(unit[0, n] + HALO, 32)
        target = pl.ds(pl.multiple_of(unit[1, n], SEG), SEG)
        offset = pl.ds(pl.multiple_of(unit[2, n], SEG), SEG)
        for p in range(4):

            @pl.when(unit[3, n] == p)
            def _():
                made = x_stack[pl.ds(rows, SEG)].astype(f32)
                total[target] += made * columns[offset, p : p + 1]

        return carry

    lax.fori_loop(0, units, gather, 0)

    def store(index, carry):
        where = pl.ds(pl.multiple_of(index * 512, 512), 512)
        sums[where] = total[where].astype(bf16)
        lent_sums[index] = total[pl.ds(pl.multiple_of(SHARD + index * 512, 512), 512)].astype(bf16)
        return carry

    lax.fori_loop(0, 4, store, 0)


def run_network(count, table, shares, feats, lent, norms, lent_norms, net, profiles):
    vmem, smem, hbm = (pl.BlockSpec(memory_space=m) for m in (pltpu.VMEM, pltpu.SMEM, pl.ANY))
    first_weight, deep_weight, layer_bias, head_weight, head_bias = net
    return pl.pallas_call(
        functools.partial(network_kernel, count),
        out_shape=[
            jax.ShapeDtypeStruct((SHARD, 128), bf16),
            jax.ShapeDtypeStruct((NSEG, SEG), f32),
            jax.ShapeDtypeStruct((4, 512, 128), bf16),
        ],
        in_specs=[smem, smem, hbm, hbm, hbm, hbm, hbm, hbm, vmem, hbm, vmem, vmem],
        out_specs=[vmem, vmem, vmem],
        scratch_shapes=[
            pltpu.VMEM((SHARD + HALO + 4 * (512 + HALO), 128), bf16),
            pltpu.VMEM((10 * SLOTS, 128), f32),
            pltpu.VMEM((384, 256), bf16),
            pltpu.VMEM((3, 768, 256), bf16),
            pltpu.VMEM((256, 128), bf16),
            pltpu.VMEM((CAPACITY + HALO, 128), bf16),
            pltpu.VMEM((CAPACITY + HALO, 256), bf16),
            pltpu.VMEM((CAPACITY + HALO, 256), bf16),
            pltpu.VMEM((2 * SHARD, 128), f32),
            pltpu.VMEM((4096, 8), f32),
            pltpu.VMEM((4 * 32, SEG), f32),
            pltpu.SMEM((4, UNITS), i32),
            pltpu.SMEM((UNITS,), i32),
            pltpu.SemaphoreType.DMA((13,)),
        ],
        compiler_params=pltpu.CompilerParams(vmem_limit_bytes=62 * 2**20),
    )(table, shares, feats, lent, norms, lent_norms, first_weight, deep_weight, layer_bias, head_weight, head_bias, profiles)


def return_kernel(lent_sums, sums, weights, out, arrived, send_sem, recv_sem):
    me = lax.axis_index("tm")
    barrier = pltpu.get_barrier_semaphore()
    for k in range(4):
        for partner in (helper(me, k), helped(me, k)):
            pl.semaphore_signal(barrier, inc=1, device_id=(partner,), device_id_type=MESH)
    pl.semaphore_wait(barrier, 8)
    copies = []
    for k in range(4):
        copy = pltpu.make_async_remote_copy(
            src_ref=lent_sums.at[k], dst_ref=arrived.at[k], send_sem=send_sem.at[k], recv_sem=recv_sem.at[k],
            device_id=(helped(me, k),), device_id_type=MESH,
        )
        copy.start()
        copies.append(copy)
    inverse = 1.0 / jnp.maximum(weights[...], 1.0)
    columns = [inverse[:, half * 128 : (half + 1) * 128].T for half in range(2)]
    for k in range(4):
        copies[k].wait()
        for part in range(4):
            row = part * 128
            column = columns[part % 2][:, 2 * k + part // 2 : 2 * k + part // 2 + 1]
            made = sums[pl.ds(512 * k + row, 128)].astype(f32) + arrived[k, pl.ds(row, 128)].astype(f32)
            out[pl.ds(512 * k + row, 128)] = (made * column).astype(bf16)


def bring_back(lent_sums, sums, weights):
    vmem = pl.BlockSpec(memory_space=pltpu.VMEM)
    return pl.pallas_call(
        return_kernel,
        out_shape=jax.ShapeDtypeStruct((SHARD, 128), bf16),
        in_specs=[pl.BlockSpec(memory_space=pl.ANY), vmem, vmem],
        out_specs=vmem,
        scratch_shapes=[
            pltpu.VMEM((4, 512, 128), bf16),
            pltpu.SemaphoreType.DMA((4,)),
            pltpu.SemaphoreType.DMA((4,)),
        ],
        compiler_params=pltpu.CompilerParams(
            collective_id=1, has_side_effects=True, vmem_limit_bytes=56 * 2**20
        ),
    )(lent_sums, sums, weights)


def per_device(
    stream, stem_weight, stem_bias, first_weight, deep_weight, layer_bias, head_weight, head_bias,
    profiles, starts, profile_index, counts,
):
    count = lax.axis_size("tm")
    feats, norms, table, shares, lent, lent_norms = make_features(
        count, starts, profile_index, counts, stream, stem_weight.reshape(7 * 128, 128), stem_bias.reshape(1, 128)
    )
    net = (
        first_weight.reshape(3 * 128, 256),
        deep_weight.reshape(3, 3 * 256, 256),
        layer_bias,
        head_weight,
        head_bias.reshape(1, 128),
    )
    sums, weights, lent_sums = run_network(count, table, shares, feats, lent, norms, lent_norms, net, profiles)
    return bring_back(lent_sums, sums, weights)


def solution(mesh):
    in_specs = (P("tm", None), P(), P(), P(), P(), P(), P(), P(), P(), P("tm"), P("tm"), P("tm"))
    return jax.shard_map(
        per_device, mesh=mesh, in_specs=in_specs, out_specs=P("tm", None), check_vma=False
    )
```

time: 146 us -> 70.5 us (0.48)
  the two profiles are of different devices: /device:TPU:107 before, /device:TPU:1 now
where the time goes in v2:
time: 70.5 us; the launch traced here: 70.3 us
  Pallas kernels  67.7 us (96%)
  local copies, waits for them, and re-layouts  1.87 us (3%)
    pallas_call x1, Pallas kernels, run_network(): pl.pallas_call(functools.partial(network_kernel, count), out_shape=[jax.S...  29.8 us
    pallas_call x1, Pallas kernels, make_features(): pl.pallas_call(functools.partial(feature_kernel, count), out_shape=[jax.S...  26.9 us
    pallas_call x1, Pallas kernels, bring_back(): pl.pallas_call(return_kernel, out_shape=jax.ShapeDtypeStruct((SHARD, 128)...  11 us
    unnamed x1, local copies, waits for them, and re-layouts  1.87 us

profile of v2, /device:TPU:1, one launch (start us, length us, event | category | flops | bytes accessed | tf_op | source)
XLA Modules:
  0.0 70.3 jit_solution(14427758869832312763)
XLA Ops:
  0.7 26.9 %shard_map.118 = (bf16[2080,128]{1,0:T(8,128)(2,1)}, f32[32,128]{1,0:T(8,128)}, s32[8,128]{1,0:T(8,128)}, s32[8,128]{1,0:T(8,128)}, bf16[4,544,128]{2,1,0:T(8,128)(2,1)}, /*index=5*/f32[4,32,128]{2,1,0:T(8,128)}) custom-call(s32[4]{0:T(128)} %starts.1, s32[4]{0:T(128)} %profile_index.1, s32[1]{0:T(128)S(6)} %copy.14.live, bf16[2048,128]{1,0:T(8,128)(2,1)} %stream.1, ...), custom_call_target="tpu_custom_call" | custom-call | tf_op jit(solution)/shard_map/pallas_call | solution.py:274
  27.5 29.8 %shard_map.119 = (bf16[2048,128]{1,0:T(8,128)(2,1)}, f32[8,256]{1,0:T(8,128)}, bf16[4,512,128]{2,1,0:T(8,128)(2,1)}) custom-call(s32[8,128]{1,0:T(8,128)} %get-tuple-element.14.table, s32[8,128]{1,0:T(8,128)} %get-tuple-element.15.shares, bf16[2080,128]{1,0:T(8,128)(2,1)} %get-tuple-element.16.feats_hbm, bf16[4,544,128]{2,1,0:T(8,128)(2,1)} %get-tuple-element.17.lent_hbm, ...), custom_call_target="tpu_custom_call" | custom-call | tf_op jit(solution)/shard_map/pallas_call | solution.py:508
  57.4 11.0 %shard_map.120 = bf16[2048,128]{1,0:T(8,128)(2,1)} custom-call(bf16[4,512,128]{2,1,0:T(8,128)(2,1)} %get-tuple-element.20.lent_sums, bf16[2048,128]{1,0:T(8,128)(2,1)} %get-tuple-element.21.sums, f32[8,256]{1,0:T(8,128)} %get-tuple-element.22.weights), custom_call_target="tpu_custom_call" | custom-call | tf_op jit(solution)/shard_map/pallas_call | solution.py:565
  68.4 1.9 %copy.15 = bf16[2048,128]{1,0:T(8,128)(2,1)} copy(bf16[2048,128]{1,0:T(8,128)(2,1)} %shard_map.120) | data formatting | bytes 1048576

commit v3 on v2

v3 whole, which is shorter than its diff:
```python
import functools
import math

import jax
import jax.numpy as jnp
from jax import lax
from jax.experimental import pallas as pl
from jax.experimental.pallas import tpu as pltpu
from jax.sharding import PartitionSpec as P

bf16, f32, i32 = jnp.bfloat16, jnp.float32, jnp.int32
MESH = pl.DeviceIdType.MESH
EPS = 1e-05
SEG = 256
HALO = 32
WSEG = 16
SHARD = 2048
NSEG = SHARD // SEG
SLOTS = 16
TAIL = 48
EDGE = TAIL + HALO
DEAD = -100000
G1 = math.sqrt(2.0 / math.pi)
G2 = G1 * 0.044715


def gelu32(v):
    half = 0.5 * v
    return half + half * jnp.tanh(v * (G1 + G2 * (v * v)))


def gelu16(v):
    v = v.astype(bf16)
    half = bf16(0.5) * v
    return half + half * jnp.tanh(v * (bf16(G1) + bf16(G2) * (v * v)))


def coordinates(d):
    return lax.div(d, 32), lax.rem(lax.div(d, 8), 4), lax.rem(lax.div(d, 2), 4), lax.rem(d, 2)


def device_at(y, z, x, core):
    return y * 32 + z * 8 + x * 2 + core


def helper(place, k):
    y, z, x, core = place
    if k == 0:
        return device_at(lax.rem(y + 1, 4), z, x, 1 - core)
    if k == 1:
        return device_at(lax.rem(y + 3, 4), z, x, core)
    if k == 2:
        return device_at(y, lax.rem(z + 1, 4), x, 1 - core)
    return device_at(y, lax.rem(z + 3, 4), x, core)


def helped(place, k):
    y, z, x, core = place
    if k == 0:
        return device_at(lax.rem(y + 3, 4), z, x, 1 - core)
    if k == 1:
        return device_at(lax.rem(y + 1, 4), z, x, core)
    if k == 2:
        return device_at(y, lax.rem(z + 3, 4), x, 1 - core)
    return device_at(y, lax.rem(z + 1, 4), x, core)


def lanes_core(v, lane):
    return jnp.where(lane % 2 == 0, pltpu.roll(v, 127, 1), pltpu.roll(v, 1, 1))


def lanes_y(v, lane, step):
    return pltpu.roll(v, 96 if step > 0 else 32, 1)


def lanes_z(v, lane, step):
    if step > 0:
        return jnp.where(lane % 32 < 24, pltpu.roll(v, 120, 1), pltpu.roll(v, 24, 1))
    return jnp.where(lane % 32 >= 8, pltpu.roll(v, 8, 1), pltpu.roll(v, 104, 1))


def at_helper(v, lane, k):
    if k == 0:
        return lanes_y(lanes_core(v, lane), lane, 1)
    if k == 1:
        return lanes_y(v, lane, -1)
    if k == 2:
        return lanes_z(lanes_core(v, lane), lane, 1)
    return lanes_z(v, lane, -1)


def at_helped(v, lane, k):
    if k == 0:
        return lanes_core(lanes_y(v, lane, -1), lane)
    if k == 1:
        return lanes_y(v, lane, 1)
    if k == 2:
        return lanes_core(lanes_z(v, lane, -1), lane)
    return lanes_z(v, lane, 1)


def share_out(rows):
    lane = lax.broadcasted_iota(i32, (8, 128), 1)
    segment = (lane * NSEG + lax.broadcasted_iota(i32, (8, 128), 0)).astype(f32)
    covering = jnp.zeros((8, 128), f32)
    for j in range(4):
        start = jnp.broadcast_to(rows[j : j + 1], (8, 128))
        for offset in range(-2, 2):
            moved = pltpu.roll(start, (-offset) % 128, 1) if offset else start
            there = jnp.logical_and(lane + offset >= 0, lane + offset < 128)
            there = jnp.logical_and(there, jnp.logical_and(segment >= moved, segment < moved + WSEG))
            covering = covering + jnp.where(there, 1.0, 0.0)
    caps = [
        jnp.broadcast_to(covering[2 * k : 2 * k + 1] + covering[2 * k + 1 : 2 * k + 2], (8, 128))
        for k in range(4)
    ]
    load = caps[0] + caps[1] + caps[2] + caps[3]
    given = [jnp.zeros((8, 128), f32) for _ in range(4)]
    for _ in range(4):
        for k in range(4):
            half = 0.5 * (load - at_helper(load, lane, k))
            move = jnp.where(half >= 0, jnp.floor(half), -jnp.floor(-half))
            move = jnp.clip(move, -given[k], caps[k] - given[k])
            given[k] = given[k] + move
            load = load - move + at_helped(move, lane, k)
    return given


def feature_kernel(
    count, starts, profile_index, live, stream, weight_hbm, bias, feats, norms, table, shares, lent, lent_norms,
    rows, weight, stats, mine, known, nearby, edge, local_sem, edge_send, edge_recv, line_send, line_recv, stat_send,
    stat_recv, known_send, known_recv,
    lent_send, lent_recv, norm_send, norm_recv,
):
    me = lax.axis_index("tm")
    place = coordinates(me)

    def at(offset):
        return lax.rem(me + offset + count, count)

    loads = [
        pltpu.make_async_copy(src, dst, local_sem.at[n])
        for n, (src, dst) in enumerate(
            (
                (stream, rows.at[pl.ds(TAIL, SHARD)]),
                (weight_hbm, weight),
                (stream.at[pl.ds(SHARD - TAIL, TAIL)], edge.at[pl.ds(2 * EDGE, TAIL)]),
                (stream.at[pl.ds(0, HALO)], edge.at[pl.ds(EDGE + TAIL, HALO)]),
            )
        )
    ]
    for copy in loads:
        copy.start()

    lane = lax.broadcasted_iota(i32, (1, 128), 1)
    line = jnp.zeros((1, 128), f32)
    for j in range(4):
        start = jnp.where(j < live[0], starts[j] // SEG, DEAD).astype(f32)
        line = jnp.where(lane == j, start, line)
        line = jnp.where(lane == 4 + j, profile_index[j].astype(f32), line)
    known[me] = line
    nearby[2] = line

    barrier = pltpu.get_barrier_semaphore()
    partners = [at(offset) for offset in (-2, -1, 1, 2)]
    partners += [lax.div(me, 8) * 8 + lax.rem(me + step, 8) for step in range(1, 8)]
    partners += [lax.rem(me + 8 * step, count) for step in range(1, 16)]
    for k in range(4):
        partners += [helper(place, k), helped(place, k)]
    for partner in partners:
        pl.semaphore_signal(barrier, inc=1, device_id=(partner,), device_id_type=MESH)

    def send(src, dst, send_sem, recv_sem, device):
        copy = pltpu.make_async_remote_copy(
            src_ref=src, dst_ref=dst, send_sem=send_sem, recv_sem=recv_sem, device_id=(device,),
            device_id_type=MESH,
        )
        copy.start()
        return copy

    def tell(first, length, index, device):
        block = known.at[pl.ds(first, length)]
        return send(block, block, known_send.at[index], known_recv.at[index], device)

    def convolved(block, length):
        wide = jnp.concatenate([block[13 + k : 13 + k + length] for k in range(7)], axis=1)
        return gelu32(jnp.dot(wide, weight[...], preferred_element_type=f32) + bias[...])

    def stem(first, length):
        block = rows[pl.ds(first + 32, length + 32)]
        feats[pl.ds(first + HALO, length)] = convolved(block, length).astype(bf16)

    def lend(k):
        return send(
            feats.at[pl.ds(512 * k, 512 + HALO)], lent.at[k], lent_send.at[k], lent_recv.at[k], helper(place, k)
        )

    pl.semaphore_wait(barrier, len(partners))
    edges = [
        send(
            stream.at[pl.ds(SHARD - TAIL, TAIL)], edge.at[pl.ds((2 - offset) * EDGE, TAIL)],
            edge_send.at[index], edge_recv.at[index], at(offset),
        )
        for index, offset in enumerate((2, 1, -1))
    ] + [
        send(
            stream.at[pl.ds(0, HALO)], edge.at[pl.ds((1 - offset) * EDGE + TAIL, HALO)],
            edge_send.at[3 + index], edge_recv.at[3 + index], at(offset),
        )
        for index, offset in enumerate((1, -1, -2))
    ]
    lines = [
        send(known.at[me], nearby.at[2 - offset], line_send.at[index], line_recv.at[index], at(offset))
        for index, offset in enumerate((2, 1, -1))
    ]
    eight = lax.div(me, 8) * 8
    near = [tell(me, 1, step - 1, eight + lax.rem(me + step, 8)) for step in range(1, 8)]
    for copy in loads:
        copy.wait()
    stem(16, 496)
    stem(512, 512)
    stem(1024, 512)
    stem(1536, 496)
    for k in range(NSEG):
        low, high = max(k * SEG, 16), min(k * SEG + SEG, SHARD - 16)
        part = feats[pl.ds(low + HALO, high - low)].astype(f32)
        for n, total in enumerate((part, part * part)):
            total = jnp.sum(total, axis=0, keepdims=True)
            mine[n, k : k + 1] = total
            stats[n, 16 + k : 17 + k] = total
    moments = [
        send(mine, stats.at[:, pl.ds(8 * (2 - offset), 8)], stat_send.at[index], stat_recv.at[index], at(offset))
        for index, offset in enumerate((-2, -1, 1, 2))
    ]
    for copy in near:
        copy.wait()
    far = [tell(eight, 8, 6 + step, lax.rem(me + 8 * step, count)) for step in range(1, 16)]
    for copy in edges:
        copy.wait()
    for b in range(4):

        @pl.when(me - 2 + b == -1)
        def _():
            edge[pl.ds(b * EDGE, TAIL)] = jnp.zeros((TAIL, 128), bf16)

        @pl.when(me - 2 + b == count - 1)
        def _():
            edge[pl.ds(b * EDGE + TAIL, HALO)] = jnp.zeros((HALO, 128), bf16)

    rows[pl.ds(0, TAIL)] = edge[pl.ds(EDGE, TAIL)]
    rows[pl.ds(SHARD + TAIL, 16)] = edge[pl.ds(2 * EDGE + TAIL, 16)]
    stem(-HALO, HALO + 16)
    stem(SHARD - 16, 16)
    loans = [lend(k) for k in range(4)]
    ends = convolved(edge[...], 4 * EDGE - 32).astype(bf16).astype(f32)
    for copy in moments + lines:
        copy.wait()
    for b in range(4):
        for side in range(2):
            part = ends[b * EDGE + 16 * (1 + side) : b * EDGE + 16 * (2 + side)]
            row = 8 * b + 7 + side
            stats[0, row : row + 1] += jnp.sum(part, axis=0, keepdims=True)
            stats[1, row : row + 1] += jnp.sum(part * part, axis=0, keepdims=True)

    row = lax.broadcasted_iota(i32, (40, 128), 0).astype(f32)
    for slot in range(SLOTS):
        start = nearby[slot // 4][:, slot % 4 : slot % 4 + 1]
        first = start - (NSEG * me - 16).astype(f32)
        covered = jnp.logical_and(row >= first, row < first + WSEG)
        mean, square = (
            jnp.sum(jnp.where(covered, stats[n], 0.0), axis=0, keepdims=True) * (1.0 / (WSEG * SEG))
            for n in range(2)
        )
        scale = lax.rsqrt(square - mean * mean + EPS)
        norms[slot : slot + 1] = scale
        norms[SLOTS + slot : SLOTS + slot + 1] = -mean * scale
    for k in range(4):
        loans.append(send(norms, lent_norms.at[k], norm_send.at[k], norm_recv.at[k], helper(place, k)))

    for copy in far:
        copy.wait()
    turned = known[...].reshape(128, 128).T[:8]
    table[...] = turned.astype(i32)
    given = share_out(turned)
    shares[...] = jnp.concatenate([given[k][:1] for k in range(4)] + [jnp.zeros((4, 128), f32)], axis=0).astype(i32)
    for copy in loans:
        copy.wait()


def make_features(count, starts, profile_index, counts, stream, weight, bias):
    vmem, smem, hbm = (pl.BlockSpec(memory_space=m) for m in (pltpu.VMEM, pltpu.SMEM, pl.ANY))
    dma = pltpu.SemaphoreType.DMA
    return pl.pallas_call(
        functools.partial(feature_kernel, count),
        out_shape=[
            jax.ShapeDtypeStruct((SHARD + HALO, 128), bf16),
            jax.ShapeDtypeStruct((2 * SLOTS, 128), f32),
            jax.ShapeDtypeStruct((8, 128), i32),
            jax.ShapeDtypeStruct((8, 128), i32),
            jax.ShapeDtypeStruct((4, 512 + HALO, 128), bf16),
            jax.ShapeDtypeStruct((4, 2 * SLOTS, 128), f32),
        ],
        in_specs=[smem, smem, smem, hbm, hbm, vmem],
        out_specs=[vmem, vmem, vmem, vmem, hbm, hbm],
        scratch_shapes=[
            pltpu.VMEM((SHARD + 64, 128), bf16),
            pltpu.VMEM((7 * 128, 128), bf16),
            pltpu.VMEM((2, 40, 128), f32),
            pltpu.VMEM((2, NSEG, 128), f32),
            pltpu.VMEM((128, 1, 128), f32),
            pltpu.VMEM((5, 1, 128), f32),
            pltpu.VMEM((4 * EDGE, 128), bf16),
            dma((4,)),
            dma((6,)), dma((6,)),
            dma((3,)), dma((3,)),
            dma((4,)), dma((4,)),
            dma((22,)), dma((22,)),
            dma((4,)), dma((4,)),
            dma((4,)), dma((4,)),
        ],
        compiler_params=pltpu.CompilerParams(
            collective_id=0, has_side_effects=True, vmem_limit_bytes=56 * 2**20
        ),
    )(starts, profile_index, counts, stream, weight, bias)


BIG = 2048
CAPACITY = 128 * SEG + 128 * HALO + BIG
UNITS = 160


def network_kernel(
    count, table, shares, feats_hbm, lent_hbm, norms_hbm, lent_norms_hbm, first_hbm, deep_hbm, layer_bias, head_hbm,
    head_bias, profiles, sums, lent_sums, feats, norms, first_weight, deep_weight, head_weight, x_stack, h_a,
    h_b, total, head_turned, padded, weights, unit, zeros, sems,
):
    me = lax.axis_index("tm")
    place = coordinates(me)
    pieces = [
        (first_hbm, first_weight),
        (deep_hbm, deep_weight),
        (head_hbm, head_weight),
        (feats_hbm, feats.at[pl.ds(0, SHARD + HALO)]),
        (norms_hbm, norms.at[pl.ds(0, 2 * SLOTS)]),
    ]
    for k in range(4):
        pieces.append((lent_hbm.at[k], feats.at[pl.ds(SHARD + HALO + (512 + HALO) * k, 512 + HALO)]))
        pieces.append((lent_norms_hbm.at[k], norms.at[pl.ds(2 * SLOTS * (k + 1), 2 * SLOTS)]))
    loads = [pltpu.make_async_copy(src, dst, sems.at[n]) for n, (src, dst) in enumerate(pieces)]
    for copy in loads[3:] + loads[:3]:
        copy.start()

    padded[...] = jnp.zeros_like(padded)
    for p in range(4):
        for k in range(WSEG):
            padded[p * 32 + 8 + k : p * 32 + 9 + k] = profiles[p : p + 1, k * SEG : (k + 1) * SEG]
    weights[...] = jnp.zeros_like(weights)

    def clear(index, carry):
        total[:, pl.ds(pl.multiple_of(index * SEG, SEG), SEG)] = jnp.zeros((128, SEG), f32)
        return carry

    lax.fori_loop(0, 2 * NSEG, clear, 0)
    for copy in loads[3:]:
        copy.wait()

    def window(home, slot):
        owner = home + slot // 4 - 2
        inside = jnp.logical_and(owner >= 0, owner < count)
        owner = jnp.clip(owner, 0, count - 1)
        start = jnp.where(inside, table[lax.rem(slot, 4), owner], DEAD)
        return start - NSEG * home, table[4 + lax.rem(slot, 4), owner]

    def put(base, target, norm, slot, rel, profile, low, high, fresh, state):
        scale = norms[pl.ds(norm + slot, 1)]
        shift = norms[pl.ds(norm + SLOTS + slot, 1)]

        def normalised(row, length):
            block = feats[pl.ds(pl.multiple_of(row, 32), length)].astype(f32)
            return (block * scale + shift).astype(bf16)

        def begin(state):
            rows, units, blanks = state
            rows = pl.multiple_of(rows, 32)

            @pl.when(low == rel)
            def _():
                x_stack[pl.ds(rows + HALO, HALO)] = jnp.zeros((HALO, 128), bf16)
                zeros[blanks] = rows + HALO

            @pl.when(low != rel)
            def _():
                x_stack[pl.ds(rows + HALO, HALO)] = normalised(base + low * SEG, HALO)

            return rows + HALO, units, blanks + jnp.where(low == rel, 1, 0)

        def segment(k, state):
            rows, units, blanks = state
            rows = pl.multiple_of(rows, 32)
            x_stack[pl.ds(rows + HALO, SEG)] = normalised(base + k * SEG + HALO, SEG)
            unit[0, units] = rows
            unit[1, units] = target + k * SEG
            unit[2, units] = profile * 32 + 8 + k - rel
            return rows + SEG, units + 1, blanks

        state = lax.cond(fresh, begin, lambda s: s, state)
        return lax.fori_loop(low, high, segment, state)

    def own_slot(slot, carry):
        rel, profile = window(me, slot)

        def covered(carry):
            for k in range(NSEG):
                weights[k : k + 1] += padded[pl.ds(profile * 32 + 8 - rel + k, 1)]
            state, lefts = carry[:3], list(carry[3:])
            end = i32(-1)
            for k in range(4):
                first = jnp.maximum(rel, 2 * k)
                high = jnp.minimum(rel + WSEG, 2 * k + 2)
                given = jnp.minimum(lefts[k], jnp.maximum(high - first, 0))
                lefts[k] = lefts[k] - given
                low = first + given
                fresh = jnp.logical_and(high > low, low != end)
                state = put(0, 0, 0, slot, rel, profile, low, high, fresh, state)
                end = jnp.where(high > low, high, end)
            return (*state, *lefts)

        return lax.cond(jnp.logical_and(rel > -WSEG, rel < NSEG), covered, lambda c: c, carry)

    carry = lax.fori_loop(0, SLOTS, own_slot, (i32(0), i32(0), i32(0), *(shares[k, me] for k in range(4))))
    state = carry[:3]
    for k in range(4):
        home = helped(place, k)
        share = shares[k, home]

        def lent_slot(slot, carry, k=k, home=home):
            rel, profile = window(home, slot)

            def covered(carry):
                for i in range(2):
                    row = NSEG + 2 * k + i
                    weights[row : row + 1] += padded[pl.ds(profile * 32 + 8 - rel + 2 * k + i, 1)]
                first = jnp.maximum(rel, 2 * k)
                taken = jnp.minimum(carry[3], jnp.maximum(jnp.minimum(rel + WSEG, 2 * k + 2) - first, 0))
                state = put(
                    SHARD + HALO + HALO * k, SHARD, 2 * SLOTS * (k + 1), slot, rel, profile, first, first + taken,
                    taken > 0, carry[:3],
                )
                return (*state, carry[3] - taken)

            return lax.cond(jnp.logical_and(rel > -WSEG, rel < NSEG), covered, lambda c: c, carry)

        state = lax.fori_loop(0, jnp.where(share > 0, SLOTS, 0), lent_slot, (*state, share))[:3]
    rows, units, blanks = state

    for copy in loads[:3]:
        copy.wait()
    sizes, spans, first = (2048, 1024, 512), [], i32(0)
    for size in sizes:
        steps = (rows - first + (size - 1 if size == sizes[-1] else 0)) // size
        spans.append((size, first, steps))
        first = first + steps * size

    def over_rows(body):
        for size, first, steps in spans:

            def step(index, carry, size=size, first=first):
                body(pl.multiple_of(first + index * size, sizes[-1]), size)
                return carry

            lax.fori_loop(0, steps, step, 0)

    def layer(index, source, target, weight):
        spread = 2**index

        def body(first, length):
            block = source[pl.ds(first, length + HALO)]
            wide = jnp.concatenate(
                [block[HALO - s * spread : HALO - s * spread + length] for s in (2, 1, 0)], axis=1
            )
            summed = jnp.dot(wide, weight, preferred_element_type=f32)
            made = gelu16(summed + layer_bias[index : index + 1])
            if index:
                made = made + block[HALO:]
            target[pl.ds(first + HALO, length)] = made

        over_rows(body)

        def blank(n, carry):
            target[pl.ds(pl.multiple_of(zeros[n], 32), HALO)] = jnp.zeros((HALO, 256), bf16)
            return carry

        lax.fori_loop(0, blanks, blank, 0)

    layer(0, x_stack, h_a, first_weight[...])
    layer(1, h_a, h_b, deep_weight[0])
    layer(2, h_b, h_a, deep_weight[1])
    layer(3, h_a, h_b, deep_weight[2])

    for extra in range(3):
        unit[0, units + extra] = unit[0, 0]
        unit[1, units + extra] = 0
        unit[2, units + extra] = 0

    for half in range(2):
        part = head_weight[pl.ds(half * 128, 128)].astype(f32)
        head_turned[:, half * 128 : (half + 1) * 128] = part.T.astype(bf16)

    def gather(n, carry):
        for u in range(4):
            rows = pl.multiple_of(unit[0, 4 * n + u] + HALO, 32)
            target = pl.ds(pl.multiple_of(unit[1, 4 * n + u], SEG), SEG)
            made = lax.dot_general(
                head_turned[...], h_b[pl.ds(rows, SEG)], (((1,), (1,)), ((), ())), preferred_element_type=f32
            )
            total[:, target] += made * padded[pl.ds(unit[2, 4 * n + u], 1)]
        return carry

    lax.fori_loop(0, (units + 3) // 4, gather, 0)

    bias = jnp.broadcast_to(head_bias[...], (8, 128)).T[:, :1]

    def store(index, carry):
        mine, lent = pl.ds(pl.multiple_of(index * SEG, SEG), SEG), pl.multiple_of(SHARD + index * SEG, SEG)
        weight = weights[pl.ds(index, 1)]
        made = (total[:, mine] + bias * weight) * (1.0 / jnp.maximum(weight, 1.0))
        sums[mine] = made.T.astype(bf16)
        weight = weights[pl.ds(NSEG + index, 1)]
        made = total[:, pl.ds(lent, SEG)] * (1.0 / jnp.maximum(weight, 1.0))
        lent_sums[mine] = made.T.astype(bf16)
        return carry

    lax.fori_loop(0, NSEG, store, 0)


def run_network(count, table, shares, feats, lent, norms, lent_norms, net, profiles):
    vmem, smem, hbm = (pl.BlockSpec(memory_space=m) for m in (pltpu.VMEM, pltpu.SMEM, pl.ANY))
    first_weight, deep_weight, layer_bias, head_weight, head_bias = net
    return pl.pallas_call(
        functools.partial(network_kernel, count),
        out_shape=[
            jax.ShapeDtypeStruct((SHARD, 128), bf16),
            jax.ShapeDtypeStruct((SHARD, 128), bf16),
        ],
        in_specs=[smem, smem, hbm, hbm, hbm, hbm, hbm, hbm, vmem, hbm, vmem, vmem],
        out_specs=[vmem, vmem],
        scratch_shapes=[
            pltpu.VMEM((SHARD + HALO + 4 * (512 + HALO), 128), bf16),
            pltpu.VMEM((10 * SLOTS, 128), f32),
            pltpu.VMEM((384, 256), bf16),
            pltpu.VMEM((3, 768, 256), bf16),
            pltpu.VMEM((256, 128), bf16),
            pltpu.VMEM((CAPACITY + HALO, 128), bf16),
            pltpu.VMEM((CAPACITY + HALO, 256), bf16),
            pltpu.VMEM((CAPACITY + HALO, 256), bf16),
            pltpu.VMEM((128, 2 * SHARD), f32),
            pltpu.VMEM((128, 256), bf16),
            pltpu.VMEM((4 * 32, SEG), f32),
            pltpu.VMEM((2 * NSEG, SEG), f32),
            pltpu.SMEM((3, UNITS), i32),
            pltpu.SMEM((UNITS,), i32),
            pltpu.SemaphoreType.DMA((13,)),
        ],
        compiler_params=pltpu.CompilerParams(vmem_limit_bytes=62 * 2**20),
    )(table, shares, feats, lent, norms, lent_norms, first_weight, deep_weight, layer_bias, head_weight, head_bias, profiles)


def return_kernel(lent_sums, arrived, send_sem, recv_sem):
    me = lax.axis_index("tm")
    place = coordinates(me)
    barrier = pltpu.get_barrier_semaphore()
    for k in range(4):
        for partner in (helper(place, k), helped(place, k)):
            pl.semaphore_signal(barrier, inc=1, device_id=(partner,), device_id_type=MESH)
    pl.semaphore_wait(barrier, 8)
    copies = []
    for k in range(4):
        rows = pl.ds(512 * k, 512)
        copy = pltpu.make_async_remote_copy(
            src_ref=lent_sums.at[rows], dst_ref=arrived.at[rows], send_sem=send_sem.at[k], recv_sem=recv_sem.at[k],
            device_id=(helped(place, k),), device_id_type=MESH,
        )
        copy.start()
        copies.append(copy)
    for copy in copies:
        copy.wait()


def bring_back(lent_sums):
    hbm = pl.BlockSpec(memory_space=pl.ANY)
    return pl.pallas_call(
        return_kernel,
        out_shape=jax.ShapeDtypeStruct((SHARD, 128), bf16),
        in_specs=[hbm],
        out_specs=hbm,
        scratch_shapes=[pltpu.SemaphoreType.DMA((4,)), pltpu.SemaphoreType.DMA((4,))],
        compiler_params=pltpu.CompilerParams(
            collective_id=1, has_side_effects=True, vmem_limit_bytes=56 * 2**20
        ),
    )(lent_sums)


def per_device(
    stream, stem_weight, stem_bias, first_weight, deep_weight, layer_bias, head_weight, head_bias,
    profiles, starts, profile_index, counts,
):
    count = lax.axis_size("tm")
    feats, norms, table, shares, lent, lent_norms = make_features(
        count, starts, profile_index, counts, stream, stem_weight.reshape(7 * 128, 128), stem_bias.reshape(1, 128)
    )
    net = (
        first_weight.reshape(3 * 128, 256),
        deep_weight.reshape(3, 3 * 256, 256),
        layer_bias,
        head_weight,
        head_bias.reshape(1, 128),
    )
    sums, lent_sums = run_network(count, table, shares, feats, lent, norms, lent_norms, net, profiles)
    return (sums.astype(f32) + bring_back(lent_sums).astype(f32)).astype(bf16)


def solution(mesh):
    in_specs = (P("tm", None), P(), P(), P(), P(), P(), P(), P(), P(), P("tm"), P("tm"), P("tm"))
    return jax.shard_map(
        per_device, mesh=mesh, in_specs=in_specs, out_specs=P("tm", None), check_vma=False
    )
```

time: 70.5 us -> 65.4 us (0.928)
  the two profiles are of different devices: /device:TPU:1 before, /device:TPU:4 now
where the time goes in v3:
time: 65.4 us; the launch traced here: 65.2 us
  Pallas kernels  62.5 us (96%)
  other arithmetic  1.97 us (3%)
  between operations  0.69 us (1%)
    pallas_call x1, Pallas kernels, run_network(): pl.pallas_call(functools.partial(network_kernel, count), out_shape=[jax.S...  32.7 us
    pallas_call x1, Pallas kernels, make_features(): pl.pallas_call(functools.partial(feature_kernel, count), out_shape=[jax.S...  20.4 us
    pallas_call x1, Pallas kernels, bring_back(): pl.pallas_call(return_kernel, out_shape=jax.ShapeDtypeStruct((SHARD, 128)...  9.43 us
    convert_element_type x1, other arithmetic, per_device(): return (sums.astype(f32) + bring_back(lent_sums).astype(f32)).astype(bf16)  1.97 us

profile of v3, /device:TPU:4, one launch (start us, length us, event | category | flops | bytes accessed | tf_op | source)
XLA Modules:
  0.0 65.2 jit_solution(12128554148933485366)
XLA Ops:
  0.7 20.4 %shard_map.118 = (bf16[2080,128]{1,0:T(8,128)(2,1)}, f32[32,128]{1,0:T(8,128)}, s32[8,128]{1,0:T(8,128)}, s32[8,128]{1,0:T(8,128)}, bf16[4,544,128]{2,1,0:T(8,128)(2,1)}, /*index=5*/f32[4,32,128]{2,1,0:T(8,128)}) custom-call(s32[4]{0:T(128)} %starts.1, s32[4]{0:T(128)} %profile_index.1, s32[1]{0:T(128)S(6)} %copy.13.live, bf16[2048,128]{1,0:T(8,128)(2,1)} %stream.1, ...), custom_call_target="tpu_custom_call" | custom-call | tf_op jit(solution)/shard_map/pallas_call | solution.py:293
  21.0 32.7 %shard_map.119 = (bf16[2048,128]{1,0:T(8,128)(2,1)}, bf16[2048,128]{1,0:T(8,128)(2,1)}) custom-call(s32[8,128]{1,0:T(8,128)} %get-tuple-element.13.table, s32[8,128]{1,0:T(8,128)} %get-tuple-element.14.shares, bf16[2080,128]{1,0:T(8,128)(2,1)} %get-tuple-element.15.feats_hbm, bf16[4,544,128]{2,1,0:T(8,128)(2,1)} %get-tuple-element.16.lent_hbm, ...), custom_call_target="tpu_custom_call" | custom-call | tf_op jit(solution)/shard_map/pallas_call | solution.py:539
  53.7 0.0 copy-start
  53.7 9.4 %shard_map.120 = bf16[2048,128]{1,0:T(8,128)(2,1)} custom-call(bf16[2048,128]{1,0:T(8,128)(2,1)} %get-tuple-element.20.lent_sums), custom_call_target="tpu_custom_call" | custom-call | tf_op jit(solution)/shard_map/pallas_call | solution.py:591
  63.2 0.0 copy-done
  63.2 2.0 %add_convert_fusion = bf16[2048,128]{1,0:T(8,128)(2,1)} fusion(bf16[2048,128]{1,0:T(8,128)(2,1)} %shard_map.120, bf16[2048,128]{1,0:T(8,128)(2,1)S(1)} %copy-done), kind=kLoop, calls=%fused_computation | loop fusion | flops 1048576 | bytes 1572864 | tf_op jit(solution)/shard_map/convert_element_type | solution.py:619
Async XLA Ops:
  53.7 9.5 %copy-start = (bf16[2048,128]{1,0:T(8,128)(2,1)S(1)}, bf16[2048,128]{1,0:T(8,128)(2,1)}, u32[]{:S(2)}) copy-start(bf16[2048,128]{1,0:T(8,128)(2,1)} %get-tuple-element.19) | copy-start | bytes 1572868

commit v4 on v3

--- a/solution.py
+++ b/solution.py
@@ -14,6 +14,7 @@
 SEG = 256
 HALO = 32
 WSEG = 16
+SWEEPS = 3
 SHARD = 2048
 NSEG = SHARD // SEG
 SLOTS = 16
@@ -116,7 +117,7 @@
     ]
     load = caps[0] + caps[1] + caps[2] + caps[3]
     given = [jnp.zeros((8, 128), f32) for _ in range(4)]
-    for _ in range(4):
+    for _ in range(SWEEPS):
         for k in range(4):
             half = 0.5 * (load - at_helper(load, lane, k))
             move = jnp.where(half >= 0, jnp.floor(half), -jnp.floor(-half))
@@ -324,9 +325,10 @@
     )(starts, profile_index, counts, stream, weight, bias)
 
 
-BIG = 2048
-CAPACITY = 128 * SEG + 128 * HALO + BIG
-UNITS = 160
+SIZES = (4608, 2304, 1152, 576)
+BATCH = 48
+CAPACITY = -(-BATCH * (SEG + HALO) // SIZES[-1]) * SIZES[-1]
+UNITS = 136
 
 
 def network_kernel(
@@ -361,8 +363,6 @@
         return carry
 
     lax.fori_loop(0, 2 * NSEG, clear, 0)
-    for copy in loads[3:]:
-        copy.wait()
 
     def window(home, slot):
         owner = home + slot // 4 - 2
@@ -371,39 +371,19 @@
         start = jnp.where(inside, table[lax.rem(slot, 4), owner], DEAD)
         return start - NSEG * home, table[4 + lax.rem(slot, 4), owner]
 
-    def put(base, target, norm, slot, rel, profile, low, high, fresh, state):
-        scale = norms[pl.ds(norm + slot, 1)]
-        shift = norms[pl.ds(norm + SLOTS + slot, 1)]
-
-        def normalised(row, length):
-            block = feats[pl.ds(pl.multiple_of(row, 32), length)].astype(f32)
-            return (block * scale + shift).astype(bf16)
-
-        def begin(state):
-            rows, units, blanks = state
-            rows = pl.multiple_of(rows, 32)
-
-            @pl.when(low == rel)
-            def _():
-                x_stack[pl.ds(rows + HALO, HALO)] = jnp.zeros((HALO, 128), bf16)
-                zeros[blanks] = rows + HALO
-
-            @pl.when(low != rel)
-            def _():
-                x_stack[pl.ds(rows + HALO, HALO)] = normalised(base + low * SEG, HALO)
-
-            return rows + HALO, units, blanks + jnp.where(low == rel, 1, 0)
-
+    def put(base, target, norm, rel, profile, low, high, fresh, state):
         def segment(k, state):
-            rows, units, blanks = state
-            rows = pl.multiple_of(rows, 32)
-            x_stack[pl.ds(rows + HALO, SEG)] = normalised(base + k * SEG + HALO, SEG)
+            rows, units = state
+            ahead = jnp.where(jnp.logical_and(k == low, fresh), jnp.where(k == rel, 2, 1), 0)
+            rows = rows + jnp.where(ahead > 0, HALO, 0)
             unit[0, units] = rows
             unit[1, units] = target + k * SEG
             unit[2, units] = profile * 32 + 8 + k - rel
-            return rows + SEG, units + 1, blanks
-
-        state = lax.cond(fresh, begin, lambda s: s, state)
+            unit[3, units] = base + k * SEG
+            unit[4, units] = norm
+            unit[5, units] = ahead
+            return rows + SEG, units + 1
+
         return lax.fori_loop(low, high, segment, state)
 
     def own_slot(slot, carry):
@@ -412,7 +392,7 @@
         def covered(carry):
             for k in range(NSEG):
                 weights[k : k + 1] += padded[pl.ds(profile * 32 + 8 - rel + k, 1)]
-            state, lefts = carry[:3], list(carry[3:])
+            state, lefts = carry[:2], list(carry[2:])
             end = i32(-1)
             for k in range(4):
                 first = jnp.maximum(rel, 2 * k)
@@ -420,15 +400,14 @@
                 given = jnp.minimum(lefts[k], jnp.maximum(high - first, 0))
                 lefts[k] = lefts[k] - given
                 low = first + given
-                fresh = jnp.logical_and(high > low, low != end)
-                state = put(0, 0, 0, slot, rel, profile, low, high, fresh, state)
+                state = put(0, 0, slot, rel, profile, low, high, low != end, state)
                 end = jnp.where(high > low, high, end)
             return (*state, *lefts)
 
         return lax.cond(jnp.logical_and(rel > -WSEG, rel < NSEG), covered, lambda c: c, carry)
 
-    carry = lax.fori_loop(0, SLOTS, own_slot, (i32(0), i32(0), i32(0), *(shares[k, me] for k in range(4))))
-    state = carry[:3]
+    carry = lax.fori_loop(0, SLOTS, own_slot, (i32(0), i32(0), *(shares[k, me] for k in range(4))))
+    state = carry[:2]
     for k in range(4):
         home = helped(place, k)
         share = shares[k, home]
@@ -441,96 +420,127 @@
                     row = NSEG + 2 * k + i
                     weights[row : row + 1] += padded[pl.ds(profile * 32 + 8 - rel + 2 * k + i, 1)]
                 first = jnp.maximum(rel, 2 * k)
-                taken = jnp.minimum(carry[3], jnp.maximum(jnp.minimum(rel + WSEG, 2 * k + 2) - first, 0))
+                taken = jnp.minimum(carry[2], jnp.maximum(jnp.minimum(rel + WSEG, 2 * k + 2) - first, 0))
                 state = put(
-                    SHARD + HALO + HALO * k, SHARD, 2 * SLOTS * (k + 1), slot, rel, profile, first, first + taken,
-                    taken > 0, carry[:3],
+                    SHARD + HALO + HALO * k, SHARD, SLOTS * (k + 1) + slot, rel, profile, first, first + taken,
+                    True, carry[:2],
                 )
-                return (*state, carry[3] - taken)
+                return (*state, carry[2] - taken)
 
             return lax.cond(jnp.logical_and(rel > -WSEG, rel < NSEG), covered, lambda c: c, carry)
 
-        state = lax.fori_loop(0, jnp.where(share > 0, SLOTS, 0), lent_slot, (*state, share))[:3]
-    rows, units, blanks = state
-
-    for copy in loads[:3]:
-        copy.wait()
-    sizes, spans, first = (2048, 1024, 512), [], i32(0)
-    for size in sizes:
-        steps = (rows - first + (size - 1 if size == sizes[-1] else 0)) // size
-        spans.append((size, first, steps))
-        first = first + steps * size
-
-    def over_rows(body):
-        for size, first, steps in spans:
-
-            def step(index, carry, size=size, first=first):
-                body(pl.multiple_of(first + index * size, sizes[-1]), size)
-                return carry
-
-            lax.fori_loop(0, steps, step, 0)
-
-    def layer(index, source, target, weight):
-        spread = 2**index
-
-        def body(first, length):
-            block = source[pl.ds(first, length + HALO)]
-            wide = jnp.concatenate(
-                [block[HALO - s * spread : HALO - s * spread + length] for s in (2, 1, 0)], axis=1
-            )
-            summed = jnp.dot(wide, weight, preferred_element_type=f32)
-            made = gelu16(summed + layer_bias[index : index + 1])
-            if index:
-                made = made + block[HALO:]
-            target[pl.ds(first + HALO, length)] = made
-
-        over_rows(body)
-
-        def blank(n, carry):
-            target[pl.ds(pl.multiple_of(zeros[n], 32), HALO)] = jnp.zeros((HALO, 256), bf16)
-            return carry
-
-        lax.fori_loop(0, blanks, blank, 0)
-
-    layer(0, x_stack, h_a, first_weight[...])
-    layer(1, h_a, h_b, deep_weight[0])
-    layer(2, h_b, h_a, deep_weight[1])
-    layer(3, h_a, h_b, deep_weight[2])
-
-    for extra in range(3):
-        unit[0, units + extra] = unit[0, 0]
-        unit[1, units + extra] = 0
-        unit[2, units + extra] = 0
-
+        state = lax.fori_loop(0, jnp.where(share > 0, SLOTS, 0), lent_slot, (*state, share))[:2]
+    rows, units = state
+    unit[0, units] = rows + HALO
+
+    for copy in loads:
+        copy.wait()
     for half in range(2):
         part = head_weight[pl.ds(half * 128, 128)].astype(f32)
         head_turned[:, half * 128 : (half + 1) * 128] = part.T.astype(bf16)
 
-    def gather(n, carry):
-        for u in range(4):
-            rows = pl.multiple_of(unit[0, 4 * n + u] + HALO, 32)
-            target = pl.ds(pl.multiple_of(unit[1, 4 * n + u], SEG), SEG)
-            made = lax.dot_general(
-                head_turned[...], h_b[pl.ds(rows, SEG)], (((1,), (1,)), ((), ())), preferred_element_type=f32
-            )
-            total[:, target] += made * padded[pl.ds(unit[2, 4 * n + u], 1)]
+    def batch(b, carry):
+        begin, end = b * BATCH, jnp.minimum(b * BATCH + BATCH, units)
+        shift = unit[0, begin] - HALO
+
+        def fill(n, blanks):
+            first = pl.multiple_of(unit[0, n] - shift, 32)
+            norm, source = unit[4, n], pl.multiple_of(unit[3, n], 32)
+            scale = norms[pl.ds(norm // SLOTS * 2 * SLOTS + norm % SLOTS, 1)]
+            offset = norms[pl.ds(norm // SLOTS * 2 * SLOTS + SLOTS + norm % SLOTS, 1)]
+            ahead = jnp.where(jnp.logical_and(n == begin, unit[5, n] == 0), 1, unit[5, n])
+
+            def normalised(row, length):
+                return (feats[pl.ds(row, length)].astype(f32) * scale + offset).astype(bf16)
+
+            x_stack[pl.ds(first + HALO, SEG)] = normalised(pl.multiple_of(source + HALO, 32), SEG)
+
+            @pl.when(ahead == 1)
+            def _():
+                x_stack[pl.ds(first, HALO)] = normalised(source, HALO)
+
+            @pl.when(ahead == 2)
+            def _():
+                x_stack[pl.ds(first, HALO)] = jnp.zeros((HALO, 128), bf16)
+                zeros[blanks] = first
+
+            return blanks + jnp.where(ahead == 2, 1, 0)
+
+        blanks = lax.fori_loop(begin, end, fill, i32(0))
+        rows = unit[0, end - 1] - shift + SEG
+        spans, first = [], i32(0)
+        for size in SIZES:
+            steps = (rows - first + (size - 1 if size == SIZES[-1] else 0)) // size
+            spans.append((size, first, steps))
+            first = first + steps * size
+        run_batch(begin, end, shift, spans, blanks)
         return carry
 
-    lax.fori_loop(0, (units + 3) // 4, gather, 0)
+    def run_batch(begin, end, shift, spans, blanks):
+        def over_rows(body):
+            for size, first, steps in spans:
+
+                def step(index, carry, size=size, first=first):
+                    body(pl.multiple_of(first + index * size, SIZES[-1]), size)
+                    return carry
+
+                lax.fori_loop(0, steps, step, 0)
+
+        def layer(index, source, target, weight):
+            spread = 2**index
+
+            def body(first, length):
+                block = source[pl.ds(first, length + HALO)]
+                width, summed = block.shape[1], layer_bias[index : index + 1]
+                for tap in range(3):
+                    at = HALO - (2 - tap) * spread
+                    part = weight[tap * width : (tap + 1) * width]
+                    summed = summed + jnp.dot(block[at : at + length], part, preferred_element_type=f32)
+                made = gelu16(summed)
+                if index:
+                    made = made + block[HALO:]
+                target[pl.ds(first + HALO, length)] = made
+
+            over_rows(body)
+
+            def blank(n, carry):
+                target[pl.ds(pl.multiple_of(zeros[n], 32), HALO)] = jnp.zeros((HALO, 256), bf16)
+                return carry
+
+            if index < 3:
+                lax.fori_loop(0, blanks, blank, 0)
+
+        layer(0, x_stack, h_a, first_weight[...])
+        layer(1, h_a, h_b, deep_weight[0])
+        layer(2, h_b, h_a, deep_weight[1])
+        layer(3, h_a, h_b, deep_weight[2])
+
+        def gather(n, carry):
+            for u in range(4):
+                index = begin + 4 * n + u
+                there = index < end
+                index = jnp.where(there, index, begin)
+                rows = pl.multiple_of(unit[0, index] - shift + HALO, 32)
+                target = pl.ds(pl.multiple_of(unit[1, index], SEG), SEG)
+                weight = padded[pl.ds(jnp.where(there, unit[2, index], 0), 1)]
+                made = lax.dot_general(
+                    head_turned[...], h_b[pl.ds(rows, SEG)], (((1,), (1,)), ((), ())), preferred_element_type=f32
+                )
+                total[:, target] += made * weight
+            return carry
+
+        lax.fori_loop(0, (end - begin + 3) // 4, gather, 0)
+
+    lax.fori_loop(0, (units + BATCH - 1) // BATCH, batch, 0)
 
     bias = jnp.broadcast_to(head_bias[...], (8, 128)).T[:, :1]
 
-    def store(index, carry):
-        mine, lent = pl.ds(pl.multiple_of(index * SEG, SEG), SEG), pl.multiple_of(SHARD + index * SEG, SEG)
-        weight = weights[pl.ds(index, 1)]
-        made = (total[:, mine] + bias * weight) * (1.0 / jnp.maximum(weight, 1.0))
-        sums[mine] = made.T.astype(bf16)
-        weight = weights[pl.ds(NSEG + index, 1)]
-        made = total[:, pl.ds(lent, SEG)] * (1.0 / jnp.maximum(weight, 1.0))
-        lent_sums[mine] = made.T.astype(bf16)
-        return carry
-
-    lax.fori_loop(0, NSEG, store, 0)
+    scale = 1.0 / jnp.maximum(weights[...], 1.0)
+    for k in range(NSEG):
+        made = total[:, k * SEG : (k + 1) * SEG] + bias * weights[k : k + 1]
+        sums[pl.ds(k * SEG, SEG)] = (made * scale[k : k + 1]).astype(bf16).T
+        lent = total[:, SHARD + k * SEG : SHARD + (k + 1) * SEG] * scale[NSEG + k : NSEG + k + 1]
+        lent_sums[pl.ds(k * SEG, SEG)] = lent.astype(bf16).T
 
 
 def run_network(count, table, shares, feats, lent, norms, lent_norms, net, profiles):
@@ -557,8 +567,8 @@
             pltpu.VMEM((128, 256), bf16),
             pltpu.VMEM((4 * 32, SEG), f32),
             pltpu.VMEM((2 * NSEG, SEG), f32),
-            pltpu.SMEM((3, UNITS), i32),
-            pltpu.SMEM((UNITS,), i32),
+            pltpu.SMEM((6, UNITS), i32),
+            pltpu.SMEM((BATCH,), i32),
             pltpu.SemaphoreType.DMA((13,)),
         ],
         compiler_params=pltpu.CompilerParams(vmem_limit_bytes=62 * 2**20),

time: 65.4 us -> 62.4 us (0.954)
  the two profiles are of different devices: /device:TPU:4 before, /device:TPU:15 now
where the time goes in v4:
time: 62.4 us; the launch traced here: 61.6 us
  Pallas kernels  58.9 us (94%)
  other arithmetic  1.97 us (3%)
  between operations  0.69 us (1%)
    pallas_call x1, Pallas kernels, run_network(): pl.pallas_call(functools.partial(network_kernel, count), out_shape=[jax.S...  30.2 us
    pallas_call x1, Pallas kernels, make_features(): pl.pallas_call(functools.partial(feature_kernel, count), out_shape=[jax.S...  19.2 us
    pallas_call x1, Pallas kernels, bring_back(): pl.pallas_call(return_kernel, out_shape=jax.ShapeDtypeStruct((SHARD, 128)...  9.49 us
    convert_element_type x1, other arithmetic, per_device(): return (sums.astype(f32) + bring_back(lent_sums).astype(f32)).astype(bf16)  1.97 us

profile of v4, /device:TPU:15, one launch (start us, length us, event | category | flops | bytes accessed | tf_op | source)
XLA Modules:
  0.0 61.6 jit_solution(8972211420726211347)
XLA Ops:
  0.7 19.2 %shard_map.118 = (bf16[2080,128]{1,0:T(8,128)(2,1)}, f32[32,128]{1,0:T(8,128)}, s32[8,128]{1,0:T(8,128)}, s32[8,128]{1,0:T(8,128)}, bf16[4,544,128]{2,1,0:T(8,128)(2,1)}, /*index=5*/f32[4,32,128]{2,1,0:T(8,128)}) custom-call(s32[4]{0:T(128)} %starts.1, s32[4]{0:T(128)} %profile_index.1, s32[1]{0:T(128)S(6)} %copy.13.live, bf16[2048,128]{1,0:T(8,128)(2,1)} %stream.1, ...), custom_call_target="tpu_custom_call" | custom-call | tf_op jit(solution)/shard_map/pallas_call | solution.py:294
  19.8 30.2 %shard_map.119 = (bf16[2048,128]{1,0:T(8,128)(2,1)}, bf16[2048,128]{1,0:T(8,128)(2,1)}) custom-call(s32[8,128]{1,0:T(8,128)} %get-tuple-element.13.table, s32[8,128]{1,0:T(8,128)} %get-tuple-element.14.shares, bf16[2080,128]{1,0:T(8,128)(2,1)} %get-tuple-element.15.feats_hbm, bf16[4,544,128]{2,1,0:T(8,128)(2,1)} %get-tuple-element.16.lent_hbm, ...), custom_call_target="tpu_custom_call" | custom-call | tf_op jit(solution)/shard_map/pallas_call | solution.py:549
  50.1 0.0 copy-start
  50.1 9.5 %shard_map.120 = bf16[2048,128]{1,0:T(8,128)(2,1)} custom-call(bf16[2048,128]{1,0:T(8,128)(2,1)} %get-tuple-element.20.lent_sums), custom_call_target="tpu_custom_call" | custom-call | tf_op jit(solution)/shard_map/pallas_call | solution.py:601
  59.6 0.0 copy-done
  59.6 2.0 %add_convert_fusion = bf16[2048,128]{1,0:T(8,128)(2,1)} fusion(bf16[2048,128]{1,0:T(8,128)(2,1)} %shard_map.120, bf16[2048,128]{1,0:T(8,128)(2,1)S(1)} %copy-done), kind=kLoop, calls=%fused_computation | loop fusion | flops 1048576 | bytes 1572864 | tf_op jit(solution)/shard_map/convert_element_type | solution.py:629
Async XLA Ops:
  50.1 9.5 %copy-start = (bf16[2048,128]{1,0:T(8,128)(2,1)S(1)}, bf16[2048,128]{1,0:T(8,128)(2,1)}, u32[]{:S(2)}) copy-start(bf16[2048,128]{1,0:T(8,128)(2,1)} %get-tuple-element.19) | copy-start | bytes 1572868

commit v5 on v4

--- a/solution.py
+++ b/solution.py
@@ -329,6 +329,7 @@
 BATCH = 48
 CAPACITY = -(-BATCH * (SEG + HALO) // SIZES[-1]) * SIZES[-1]
 UNITS = 136
+TOGETHER = 6
 
 
 def network_kernel(
@@ -492,10 +493,14 @@
             def body(first, length):
                 block = source[pl.ds(first, length + HALO)]
                 width, summed = block.shape[1], layer_bias[index : index + 1]
-                for tap in range(3):
-                    at = HALO - (2 - tap) * spread
-                    part = weight[tap * width : (tap + 1) * width]
-                    summed = summed + jnp.dot(block[at : at + length], part, preferred_element_type=f32)
+                shifted = [block[HALO - s * spread : HALO - s * spread + length] for s in (2, 1, 0)]
+                if index == 0:
+                    shifted = [jnp.concatenate(shifted[:2], axis=1), shifted[2]]
+                start = 0
+                for rows_of in shifted:
+                    part = weight[start : start + rows_of.shape[1]]
+                    start = start + rows_of.shape[1]
+                    summed = summed + jnp.dot(rows_of, part, preferred_element_type=f32)
                 made = gelu16(summed)
                 if index:
                     made = made + block[HALO:]
@@ -516,8 +521,8 @@
         layer(3, h_a, h_b, deep_weight[2])
 
         def gather(n, carry):
-            for u in range(4):
-                index = begin + 4 * n + u
+            for u in range(TOGETHER):
+                index = begin + TOGETHER * n + u
                 there = index < end
                 index = jnp.where(there, index, begin)
                 rows = pl.multiple_of(unit[0, index] - shift + HALO, 32)
@@ -529,7 +534,7 @@
                 total[:, target] += made * weight
             return carry
 
-        lax.fori_loop(0, (end - begin + 3) // 4, gather, 0)
+        lax.fori_loop(0, (end - begin + TOGETHER - 1) // TOGETHER, gather, 0)
 
     lax.fori_loop(0, (units + BATCH - 1) // BATCH, batch, 0)
 

time: 62.4 us -> 61 us (0.978)
  Pallas kernels: 58.9 us -> 57.7 us
    pallas_call x1, Pallas kernels: 30.2 us -> 28.7 us  [run_network(): pl.pallas_call(functools.partial(network_kernel, count), out_shape=[jax.S...]
where the time goes in v5:
time: 61 us; the launch traced here: 60.4 us
  Pallas kernels  57.7 us (95%)
  other arithmetic  1.97 us (3%)
  between operations  0.69 us (1%)
    pallas_call x1, Pallas kernels, run_network(): pl.pallas_call(functools.partial(network_kernel, count), out_shape=[jax.S...  28.7 us
    pallas_call x1, Pallas kernels, make_features(): pl.pallas_call(functools.partial(feature_kernel, count), out_shape=[jax.S...  19.2 us
    pallas_call x1, Pallas kernels, bring_back(): pl.pallas_call(return_kernel, out_shape=jax.ShapeDtypeStruct((SHARD, 128)...  9.88 us
    convert_element_type x1, other arithmetic, per_device(): return (sums.astype(f32) + bring_back(lent_sums).astype(f32)).astype(bf16)  1.97 us

profile of v5, /device:TPU:15, one launch (start us, length us, event | category | flops | bytes accessed | tf_op | source)
XLA Modules:
  0.0 60.4 jit_solution(8658418222557019093)
XLA Ops:
  0.7 19.2 %shard_map.118 = (bf16[2080,128]{1,0:T(8,128)(2,1)}, f32[32,128]{1,0:T(8,128)}, s32[8,128]{1,0:T(8,128)}, s32[8,128]{1,0:T(8,128)}, bf16[4,544,128]{2,1,0:T(8,128)(2,1)}, /*index=5*/f32[4,32,128]{2,1,0:T(8,128)}) custom-call(s32[4]{0:T(128)} %starts.1, s32[4]{0:T(128)} %profile_index.1, s32[1]{0:T(128)S(6)} %copy.13.live, bf16[2048,128]{1,0:T(8,128)(2,1)} %stream.1, ...), custom_call_target="tpu_custom_call" | custom-call | tf_op jit(solution)/shard_map/pallas_call | solution.py:294
  19.8 28.7 %shard_map.119 = (bf16[2048,128]{1,0:T(8,128)(2,1)}, bf16[2048,128]{1,0:T(8,128)(2,1)}) custom-call(s32[8,128]{1,0:T(8,128)} %get-tuple-element.13.table, s32[8,128]{1,0:T(8,128)} %get-tuple-element.14.shares, bf16[2080,128]{1,0:T(8,128)(2,1)} %get-tuple-element.15.feats_hbm, bf16[4,544,128]{2,1,0:T(8,128)(2,1)} %get-tuple-element.16.lent_hbm, ...), custom_call_target="tpu_custom_call" | custom-call | tf_op jit(solution)/shard_map/pallas_call | solution.py:554
  48.5 0.0 copy-start
  48.5 9.9 %shard_map.120 = bf16[2048,128]{1,0:T(8,128)(2,1)} custom-call(bf16[2048,128]{1,0:T(8,128)(2,1)} %get-tuple-element.20.lent_sums), custom_call_target="tpu_custom_call" | custom-call | tf_op jit(solution)/shard_map/pallas_call | solution.py:606
  58.4 0.0 copy-done
  58.4 2.0 %add_convert_fusion = bf16[2048,128]{1,0:T(8,128)(2,1)} fusion(bf16[2048,128]{1,0:T(8,128)(2,1)} %shard_map.120, bf16[2048,128]{1,0:T(8,128)(2,1)S(1)} %copy-done), kind=kLoop, calls=%fused_computation | loop fusion | flops 1048576 | bytes 1572864 | tf_op jit(solution)/shard_map/convert_element_type | solution.py:634
Async XLA Ops:
  48.5 9.9 %copy-start = (bf16[2048,128]{1,0:T(8,128)(2,1)S(1)}, bf16[2048,128]{1,0:T(8,128)(2,1)}, u32[]{:S(2)}) copy-start(bf16[2048,128]{1,0:T(8,128)(2,1)} %get-tuple-element.19) | copy-start | bytes 1572868

commit v6 on v5

--- a/solution.py
+++ b/solution.py
@@ -197,6 +197,8 @@
         )
 
     pl.semaphore_wait(barrier, len(partners))
+    eight = lax.div(me, 8) * 8
+    near = [tell(me, 1, step - 1, eight + lax.rem(me + step, 8)) for step in range(1, 8)]
     edges = [
         send(
             stream.at[pl.ds(SHARD - TAIL, TAIL)], edge.at[pl.ds((2 - offset) * EDGE, TAIL)],
@@ -214,8 +216,6 @@
         send(known.at[me], nearby.at[2 - offset], line_send.at[index], line_recv.at[index], at(offset))
         for index, offset in enumerate((2, 1, -1))
     ]
-    eight = lax.div(me, 8) * 8
-    near = [tell(me, 1, step - 1, eight + lax.rem(me + step, 8)) for step in range(1, 8)]
     for copy in loads:
         copy.wait()
     stem(16, 496)
@@ -325,7 +325,7 @@
     )(starts, profile_index, counts, stream, weight, bias)
 
 
-SIZES = (4608, 2304, 1152, 576)
+SIZES = (4608, 2304, 1152, 576, 288)
 BATCH = 48
 CAPACITY = -(-BATCH * (SEG + HALO) // SIZES[-1]) * SIZES[-1]
 UNITS = 136

time: 61 us -> 60.6 us (level)
    pallas_call x1, Pallas kernels: 9.88 us -> 8.43 us  [bring_back(): pl.pallas_call(return_kernel, out_shape=jax.ShapeDtypeStruct((SHARD, 128)...]
    pallas_call x1, Pallas kernels: 28.7 us -> 29.7 us  [run_network(): pl.pallas_call(functools.partial(network_kernel, count), out_shape=[jax.S...]
where the time goes in v6:
time: 60.6 us; the launch traced here: 60 us
  Pallas kernels  57.3 us (95%)
  other arithmetic  1.97 us (3%)
  between operations  0.69 us (1%)
    pallas_call x1, Pallas kernels, run_network(): pl.pallas_call(functools.partial(network_kernel, count), out_shape=[jax.S...  29.7 us
    pallas_call x1, Pallas kernels, make_features(): pl.pallas_call(functools.partial(feature_kernel, count), out_shape=[jax.S...  19.1 us
    pallas_call x1, Pallas kernels, bring_back(): pl.pallas_call(return_kernel, out_shape=jax.ShapeDtypeStruct((SHARD, 128)...  8.43 us
    convert_element_type x1, other arithmetic, per_device(): return (sums.astype(f32) + bring_back(lent_sums).astype(f32)).astype(bf16)  1.97 us

profile of v6, /device:TPU:15, one launch (start us, length us, event | category | flops | bytes accessed | tf_op | source)
XLA Modules:
  0.0 60.0 jit_solution(16086642957961202860)
XLA Ops:
  0.7 19.1 %shard_map.118 = (bf16[2080,128]{1,0:T(8,128)(2,1)}, f32[32,128]{1,0:T(8,128)}, s32[8,128]{1,0:T(8,128)}, s32[8,128]{1,0:T(8,128)}, bf16[4,544,128]{2,1,0:T(8,128)(2,1)}, /*index=5*/f32[4,32,128]{2,1,0:T(8,128)}) custom-call(s32[4]{0:T(128)} %starts.1, s32[4]{0:T(128)} %profile_index.1, s32[1]{0:T(128)S(6)} %copy.13.live, bf16[2048,128]{1,0:T(8,128)(2,1)} %stream.1, ...), custom_call_target="tpu_custom_call" | custom-call | tf_op jit(solution)/shard_map/pallas_call | solution.py:294
  19.8 29.7 %shard_map.119 = (bf16[2048,128]{1,0:T(8,128)(2,1)}, bf16[2048,128]{1,0:T(8,128)(2,1)}) custom-call(s32[8,128]{1,0:T(8,128)} %get-tuple-element.13.table, s32[8,128]{1,0:T(8,128)} %get-tuple-element.14.shares, bf16[2080,128]{1,0:T(8,128)(2,1)} %get-tuple-element.15.feats_hbm, bf16[4,544,128]{2,1,0:T(8,128)(2,1)} %get-tuple-element.16.lent_hbm, ...), custom_call_target="tpu_custom_call" | custom-call | tf_op jit(solution)/shard_map/pallas_call | solution.py:554
  49.5 0.0 copy-start
  49.5 8.4 %shard_map.120 = bf16[2048,128]{1,0:T(8,128)(2,1)} custom-call(bf16[2048,128]{1,0:T(8,128)(2,1)} %get-tuple-element.20.lent_sums), custom_call_target="tpu_custom_call" | custom-call | tf_op jit(solution)/shard_map/pallas_call | solution.py:606
  58.0 0.0 copy-done
  58.0 2.0 %add_convert_fusion = bf16[2048,128]{1,0:T(8,128)(2,1)} fusion(bf16[2048,128]{1,0:T(8,128)(2,1)} %shard_map.120, bf16[2048,128]{1,0:T(8,128)(2,1)S(1)} %copy-done), kind=kLoop, calls=%fused_computation | loop fusion | flops 1048576 | bytes 1572864 | tf_op jit(solution)/shard_map/convert_element_type | solution.py:634
Async XLA Ops:
  49.5 8.5 %copy-start = (bf16[2048,128]{1,0:T(8,128)(2,1)S(1)}, bf16[2048,128]{1,0:T(8,128)(2,1)}, u32[]{:S(2)}) copy-start(bf16[2048,128]{1,0:T(8,128)(2,1)} %get-tuple-element.19) | copy-start | bytes 1572868
